TPU v7x, 128 devices: a whole 4x4x4 slice. The times are simulated.
128 devices in a mesh: region: 4 (over x), inner: 32 (over z, y, core).
Axes of the slice: x: 4, y: 4, z: 4, core: 2. Of those that a mesh axis runs over, the one named last changes fastest.
Arguments:
- coarse_state: float32 [5, 64, 512, 128], P(None, 'region', 'inner'), may hold values from -6 to 6
- fine_state: float32 [128, 5, 32, 1024], P(('region', 'inner')), may hold values from -6 to 6
- coarse_rate: float32 [64, 512, 128], P('region', 'inner'), may hold values from 0.5 to 4
- fine_rate: float32 [128, 32, 1024], P(('region', 'inner')), may hold values from 0.5 to 4
- parents: int32 [4, 32], P('region'), may hold values from 0 to 255, as said below
- burn_steps: int32 [128], P(('region', 'inner')), may hold values from 1 to 8, as said below
Outputs:
- coarse_new: float32 [5, 64, 512, 128], P(None, 'region', 'inner')
- fine_new: float32 [128, 5, 32, 1024], P(('region', 'inner'))
Inputs may be any that keep to these rules, and one draw needn't show every extreme that they name: `parents`: each row lists 32 different blocks of its region; block b lies on inner index b // 8. At most 2 listed blocks lie on one inner index, and exactly 2 on some. `burn_steps`: some patch takes 8 sub-steps.
All inputs are finite; a program needn't handle non-finite values.
Results may differ from a plain program's by a relative error of at most 0.0003.
Values sent between devices are 32-bit elements; how exact they have to be, the bound alone decides.
A program may use at most 128 MiB of HBM per device.

v0:
```python
import functools

import jax
import jax.numpy as jnp
from jax import lax
from jax.experimental import pallas as pl
from jax.experimental.pallas import tpu as pltpu
from jax.sharding import PartitionSpec as P

MESH = pl.DeviceIdType.MESH
F32 = jnp.float32
ADV = (0.5, -0.3, 0.2)
KEEP = 0.1
NB = 0.15
BURN_MAX = 8
REGIONS = 4
INNER = 32


def iota(shape, axis):
    return lax.broadcasted_iota(jnp.int32, shape, axis)


def lanes(q, shift):
    return pltpu.roll(q, shift % 128, 1)


def rows(q, shift):
    return pltpu.roll(q, shift % q.shape[0], 0)


def hydro(c, xm, xp, yd, yu, zd, zu):
    p, u, v, w, f = c
    sx, mx = xm[0] + xm[1], xp[0] - xp[1]
    sy, my = yd(p + v), yu(p - v)
    sz, mz = zd(p + w), zu(p - w)
    hp = (sx + mx) + (sy + my) + (sz + mz)
    hu = (sx - mx) + (yd(u) + yu(u)) + (zd(u) + zu(u))
    hv = (xm[2] + xp[2]) + (sy - my) + (zd(v) + zu(v))
    hw = (xm[3] + xp[3]) + (yd(w) + yu(w)) + (sz - mz)
    hf = (
        ((1 + ADV[0]) * xm[4] + (1 - ADV[0]) * xp[4])
        + ((1 + ADV[1]) * yd(f) + (1 - ADV[1]) * yu(f))
        + ((1 + ADV[2]) * zd(f) + (1 - ADV[2]) * zu(f))
    )
    return [KEEP * a + NB * b for a, b in zip(c, (hp, hu, hv, hw, hf))]


def take(q, index):
    return jnp.take_along_axis(q, index, axis=1, mode="promise_in_bounds")


def coarse_shifts(shape):
    row, lane = iota(shape, 0), iota(shape, 1)
    zd = lambda q: jnp.where(lane == 0, 0.0, lanes(q, 1))
    zu = lambda q: jnp.where(lane == 127, 0.0, lanes(q, -1))
    yd = lambda q: jnp.where(row == 0, 0.0, rows(q, 1))
    yu = lambda q: jnp.where(row == shape[0] - 1, 0.0, rows(q, -1))
    return yd, yu, zd, zu


def fine_shifts():
    sub, lane = iota((8, 128), 0), iota((8, 128), 1)
    z = lane % 32

    def yd(q):
        t = lanes(q, 32)
        t = jnp.where(lane < 32, rows(t, 1), t)
        return jnp.where((lane < 32) & (sub == 0), 0.0, t)

    def yu(q):
        t = lanes(q, -32)
        t = jnp.where(lane >= 96, rows(t, -1), t)
        return jnp.where((lane >= 96) & (sub == 7), 0.0, t)

    zd = lambda q: jnp.where(z == 0, 0.0, lanes(q, 1))
    zu = lambda q: jnp.where(z == 31, 0.0, lanes(q, -1))
    return yd, yu, zd, zu


def burn_once(p, f, rate):
    burned = f * pl.reciprocal(1.0 + 0.5 * rate * (1.0 + 0.5 * jnp.tanh(p)), approx=True)
    return p + 0.5 * (f - burned), burned


def face_values(p, n, t1, t2, f, axis, high):
    sign = -1.0 if high else 1.0
    return [NB * (p + sign * n), NB * t1, NB * t2, NB * (1 + sign * ADV[axis]) * f]


def ghost_step(near, far, own, dlo, dhi, rate, axis, high):
    n, r = (1, 2) if axis == 0 else (2, 1)
    row, lane = iota((16, 128), 0), iota((16, 128), 1)
    an, ar, az = ADV[axis], ADV[1 - axis], ADV[2]
    minus, plus = (own, far) if high else (far, own)
    p, w, f = near[0], near[3], near[4]

    def rd(q, d):
        return jnp.where(row == 0, d, rows(q, 1))

    def ru(q, d):
        return jnp.where(row == 15, d, rows(q, -1))

    zd = lambda q: jnp.where(lane == 0, 0.0, lanes(q, 1))
    zu = lambda q: jnp.where(lane == 127, 0.0, lanes(q, -1))
    sn, mn = minus[0] + minus[n], plus[0] - plus[n]
    sr, mr = rd(p + near[r], dlo[0] + dlo[r]), ru(p - near[r], dhi[0] - dhi[r])
    sz, mz = zd(p + w), zu(p - w)
    hp = (sn + mn) + (sr + mr) + (sz + mz)
    hn = (sn - mn) + (rd(near[n], dlo[n]) + ru(near[n], dhi[n])) + (zd(near[n]) + zu(near[n]))
    hr = (minus[r] + plus[r]) + (sr - mr) + (zd(near[r]) + zu(near[r]))
    hw = (minus[3] + plus[3]) + (rd(w, dlo[3]) + ru(w, dhi[3])) + (sz - mz)
    hf = (
        ((1 + an) * minus[4] + (1 - an) * plus[4])
        + ((1 + ar) * rd(f, dlo[4]) + (1 - ar) * ru(f, dhi[4]))
        + ((1 + az) * zd(f) + (1 - az) * zu(f))
    )
    pressure, normal, tangent, across, fuel = (
        KEEP * a + NB * b for a, b in zip((p, near[n], near[r], w, f), (hp, hn, hr, hw, hf))
    )
    pressure, fuel = burn_once(pressure, fuel, rate)
    return face_values(pressure, normal, tangent, across, fuel, axis, high)


def kernel(
    coarse, fine, crate, frate, parents, steps, coarse_out, fine_out,
    c, h, cr, xh, xr, ys, yh, ds, dr, fv, zv, table, keys, p1, r1a, r1b, p2, r2a, r2b, f0, f1, fa, fb, fr, gt, ey,
    mb, r3, p4, r4, ssem, rsem, lsem, tsem,
):
    r1, r2 = (r1a, r1b), (r2a, r2b)
    region, me = lax.axis_index("region"), lax.axis_index("inner")
    up, down = lax.rem(region + 1, REGIONS), lax.rem(region + REGIONS - 1, REGIONS)
    right, left = lax.rem(me + 1, INNER), lax.rem(me + INNER - 1, INNER)
    plane, mine = (me // 8) * 8, lax.rem(me, 8)
    sub, lane = iota((8, 128), 0), iota((8, 128), 1)

    loads = [
        pltpu.make_async_copy(coarse, c.at[:, pl.ds(16, 256)], lsem.at[0]),
        pltpu.make_async_copy(crate, cr, lsem.at[1]),
    ]
    for j in range(8):
        cut = pl.ds(j * 128, 128)
        loads.append(pltpu.make_async_copy(fine.at[:, :, cut], f0.at[:, pl.ds(1, 32), j], lsem.at[2 + j]))
        loads.append(pltpu.make_async_copy(frate.at[:, cut], fr.at[:, j], lsem.at[10 + j]))
    for load in loads:
        load.start()
    barrier = pltpu.get_barrier_semaphore()

    def greet(k, carry):
        pl.semaphore_signal(
            barrier, inc=1, device_id=(region, lax.rem(me + 1 + k, INNER)), device_id_type=MESH
        )
        return carry

    lax.fori_loop(0, INNER - 1, greet, 0)
    others = [(up, me), (down, me), (up, right), (up, left), (down, right), (down, left)]
    for other in others:
        pl.semaphore_signal(barrier, inc=1, device_id=other, device_id_type=MESH)

    block_row = jnp.broadcast_to(parents[...], (32, 32))
    ri, ci = iota((32, 32), 0), iota((32, 32), 1)
    block = jnp.sum(jnp.where(ri == ci, block_row, 0), axis=1, keepdims=True)
    owner = block >> 3
    slot = jnp.sum(
        jnp.where((jnp.broadcast_to(owner, (32, 32)) == (block_row >> 3)) & (ci < ri), 1, 0),
        axis=1,
        keepdims=True,
    )
    key = jnp.broadcast_to(owner * 2 + slot, (32, 128))
    ri, ci = iota((32, 128), 0), iota((32, 128), 1)
    layer = jnp.broadcast_to((block & 7) + 1, (32, 128))
    key_row = jnp.sum(jnp.where(ri == ci, key, 0), axis=0, keepdims=True)
    patch_row = jnp.sum(jnp.where(key == ci, ri, 0), axis=0, keepdims=True)
    layer_row = jnp.sum(jnp.where(key == ci, layer, 0), axis=0, keepdims=True) - 1
    table[...] = jnp.where(
        sub == 0,
        jnp.broadcast_to(key_row, (8, 128)),
        jnp.where(sub == 1, jnp.broadcast_to(patch_row, (8, 128)), jnp.broadcast_to(layer_row, (8, 128))),
    )
    look = pltpu.make_async_copy(table, keys, tsem)
    look.start()

    zero = jnp.zeros((8, 128), F32)
    for i in range(5):
        c[i, 0:16] = jnp.zeros((16, 128), F32)
        c[i, 272:288] = jnp.zeros((16, 128), F32)
        for a in (0, 33):
            f0[i, a] = zero
            f1[i, a] = zero
    loads[0].wait()
    loads[1].wait()
    for side, (near, far) in enumerate(((15, 14), (0, 1))):
        for half in range(2):
            dst = pl.ds(half * 8, 8)
            for i in range(5):
                ys[side, i, dst] = c[i, pl.ds(16 + half * 128 + near, 8, stride=16)]
                ys[side, 6 + i, dst] = c[i, pl.ds(16 + half * 128 + far, 8, stride=16)]
            ys[side, 5, dst] = cr[pl.ds(half * 128 + near, 8, stride=16)]
    for n, at in enumerate((255, 240, 15, 0)):
        for i in range(5):
            ds[n, i : i + 1] = c[i, 16 + at : 17 + at]
        ds[n, 5:8] = jnp.zeros((3, 128), F32)

    pl.semaphore_wait(barrier, INNER - 1 + len(others))

    def remote(src, dst, n, to):
        return pltpu.make_async_remote_copy(
            src_ref=src, dst_ref=dst, send_sem=ssem.at[n], recv_sem=rsem.at[n], device_id=to, device_id_type=MESH
        )

    halos = [
        remote(ds.at[0], dr.at[0], 0, (up, right)),
        remote(ds.at[1], dr.at[1], 1, (up, left)),
        remote(ds.at[2], dr.at[2], 2, (down, right)),
        remote(ds.at[3], dr.at[3], 3, (down, left)),
        remote(ys.at[0], yh.at[0], 4, (region, right)),
        remote(ys.at[1], yh.at[1], 5, (region, left)),
        remote(c.at[:, pl.ds(16 + 224, 32)], xh.at[0], 6, (up, me)),
        remote(c.at[:, pl.ds(16, 32)], xh.at[1], 7, (down, me)),
        remote(cr.at[pl.ds(240, 16)], xr.at[0], 8, (up, me)),
        remote(cr.at[pl.ds(0, 16)], xr.at[1], 9, (down, me)),
    ]
    for halo in halos:
        halo.start()

    shifts = coarse_shifts((16, 128))

    def coarse_plane(x, carry):
        at = pl.multiple_of(x * 16, 16)
        cells = [c[i, pl.ds(at + 16, 16)] for i in range(5)]
        below = [c[i, pl.ds(at, 16)] for i in range(5)]
        above = [c[i, pl.ds(at + 32, 16)] for i in range(5)]
        for i, q in enumerate(hydro(cells, below, above, *shifts)):
            h[i, pl.ds(at, 16)] = q
        return carry

    lax.fori_loop(0, 16, coarse_plane, 0)

    look.wait()
    slots = [keys[2, 2 * me], keys[2, 2 * me + 1]]
    my_key = keys[0, me]

    side = lane % 2
    code = ((lane % 64) // 4) * 4 + (lane // 64) * 2 + (lane % 4) // 2
    picks = [lax.rem(jnp.where(side == 0, 16 * s + 127, 16 * s + 16) + 128, 128) for s in slots]
    cuts = [16 * jnp.maximum(s, 0) + lane % 16 for s in slots]
    inside = [
        jnp.where(((side == 0) & (s == 0)) | ((side == 1) & (s == 7)), 0.0, 1.0) for s in slots
    ]

    def z_values(src, base):
        low = iota((16, 128), 1) % 16 == 15

        def body(x, carry):
            at = pl.multiple_of(x * 16, 16)
            p, u, v, w, f = (src[i, pl.ds(at + base, 16)] for i in range(5))
            zv[0, pl.ds(at, 16)] = NB * (p + jnp.where(low, w, -w))
            zv[1, pl.ds(at, 16)] = NB * u
            zv[2, pl.ds(at, 16)] = NB * v
            zv[3, pl.ds(at, 16)] = f * jnp.where(low, NB * (1 + ADV[2]), NB * (1 - ADV[2]))
            return carry

        lax.fori_loop(0, 16, body, 0)

    def z_tiles():
        def body(x, tiles):
            tiles = list(tiles)
            for v in range(4):
                for odd in range(2):
                    q = zv[v, pl.ds(x * 16 + odd, 8, stride=2)]
                    here = code == x * 4 + (v % 2) * 2 + odd
                    for s in range(2):
                        tiles[s * 2 + v // 2] = jnp.where(here, take(q, picks[s]), tiles[s * 2 + v // 2])
            return tuple(tiles)

        tiles = lax.fori_loop(0, 16, body, (zero,) * 4)
        return [[tiles[s * 2 + w] * inside[s] for w in range(2)] for s in range(2)]

    def xy_tile(face, s):
        tile = zero
        for v in range(4):
            for odd in range(2):
                pos = v * 32 + odd * 16
                q = fv[face, v, pl.ds(odd, 8, stride=2)]
                tile = jnp.where(lane // 16 == pos // 16, take(q, cuts[s]), tile)
        return tile

    def put_tile(t, s, face, tile):
        p1[t, pl.ds(s * 8 + face, 8, stride=16)] = tile

    def get_tile(t, s, face):
        return p1[t, pl.ds(s * 8 + face, 8, stride=16)]

    for t in range(2):
        for s in range(2):
            for face in (6, 7):
                put_tile(t, s, face, zero)

    z_values(c, 16)
    for s, pair in enumerate(z_tiles()):
        for w, tile in enumerate(pair):
            put_tile(0, s, 4 + w, tile)

    for halo in halos:
        halo.wait_recv()
    mx = [jnp.where(region > 0, 1.0, 0.0), jnp.where(region < REGIONS - 1, 1.0, 0.0)]
    my = [jnp.where(me > 0, 1.0, 0.0), jnp.where(me < INNER - 1, 1.0, 0.0)]

    def near_x(e):
        return [xh[e, i, pl.ds(16 - 16 * e, 16)] for i in range(5)]

    def near_y(e):
        return [yh[e, i] for i in range(5)]

    for e in range(2):
        p, u, v, w, f = near_x(e)
        for i, q in enumerate(face_values(p, u, v, w, f, 0, e == 1)):
            fv[e, i] = mx[e] * q
        p, u, v, w, f = near_y(e)
        for i, q in enumerate(face_values(p, v, u, w, f, 1, e == 1)):
            fv[2 + e, i] = my[e] * q
    for s in range(2):
        for face in range(4):
            put_tile(0, s, face, xy_tile(face, s))

    def send_pieces(t):
        r1[t][mine] = p1[t, pl.ds(mine * 16, 16)]

        def body(k, carry):
            to = lax.rem(mine + 1 + k, 8)
            remote(
                p1.at[t, pl.ds(to * 16, 16)], r1[t].at[mine], 10 + t, (region, plane + to)
            ).start()
            return carry

        lax.fori_loop(0, 7, body, 0)

    def far_first(k):
        return lax.rem(me + 1 + lax.rem(15 + k, INNER - 1), INNER)

    send_pieces(0)

    def add_face(ref, cut, face, n, t1, high):
        e0, e1, e2, e3 = (fv[face, v, pl.ds(8 * cut[0], 8)] for v in range(4))
        at = cut[1]
        ref[0, at] = ref[0, at] + e0
        ref[n, at] = ref[n, at] - e0 if high else ref[n, at] + e0
        ref[t1, at] = ref[t1, at] + e1
        ref[3, at] = ref[3, at] + e2
        ref[4, at] = ref[4, at] + e3

    for half in range(2):
        add_face(h, (half, pl.ds(half * 8, 8)), 0, 1, 2, False)
        add_face(h, (half, pl.ds(240 + half * 8, 8)), 1, 1, 2, True)
        add_face(h, (half, pl.ds(half * 128, 8, stride=16)), 2, 2, 1, False)
        add_face(h, (half, pl.ds(half * 128 + 15, 8, stride=16)), 3, 2, 1, True)

    def coarse_burn(x, carry):
        at = pl.multiple_of(x * 64, 64)
        p, f = burn_once(h[0, pl.ds(at, 64)], h[4, pl.ds(at, 64)], cr[pl.ds(at, 64)])
        h[0, pl.ds(at, 64)] = p
        h[4, pl.ds(at, 64)] = f
        return carry

    lax.fori_loop(0, 4, coarse_burn, 0)

    def own_rows(axis, e):
        if axis == 0:
            return [c[i, pl.ds(16 + 240 * e, 16)] for i in range(5)]
        return [
            jnp.concatenate([c[i, pl.ds(16 + 128 * b + 15 * e, 8, stride=16)] for b in range(2)], axis=0)
            for i in range(5)
        ]

    def corner(n, scale):
        return [dr[n, i : i + 1] * scale for i in range(5)]

    for e in range(2):
        far = [xh[e, i, pl.ds(16 * e, 16)] for i in range(5)]
        values = ghost_step(
            near_x(e), far, own_rows(0, e), corner(2 * e, my[0]), corner(2 * e + 1, my[1]), xr[e], 0, e == 1
        )
        for i, q in enumerate(values):
            fv[e, i] = mx[e] * q
        far = [yh[e, 6 + i] for i in range(5)]
        values = ghost_step(
            near_y(e), far, own_rows(1, e), corner(e, mx[0]), corner(2 + e, mx[1]), yh[e, 5], 1, e == 1
        )
        for i, q in enumerate(values):
            fv[2 + e, i] = my[e] * q
    z_values(h, 0)
    for s, pair in enumerate(z_tiles()):
        for w, tile in enumerate(pair):
            put_tile(1, s, 4 + w, 0.5 * (get_tile(0, s, 4 + w) + tile))
        for face in range(4):
            put_tile(1, s, face, 0.5 * (get_tile(0, s, face) + xy_tile(face, s)))
    send_pieces(1)

    for load in loads[2:]:
        load.wait()
    count = steps[0]
    counted = jnp.broadcast_to(count, (8, 128)).astype(F32)
    span = 0.25 / counted
    fine_shift = fine_shifts()

    def rates(x, carry):
        q = span * fr[x]
        fa[x] = 1.0 + q
        fb[x] = 0.5 * q
        return carry

    lax.fori_loop(0, 32, rates, 0)

    def fine_hydro(src, dst):
        def body(x, carry):
            cells = [src[i, x + 1] for i in range(5)]
            below = [src[i, x] for i in range(5)]
            above = [src[i, x + 2] for i in range(5)]
            for i, q in enumerate(hydro(cells, below, above, *fine_shift)):
                dst[i, x + 1] = q
            return carry

        lax.fori_loop(0, 32, body, 0)

    fine_hydro(f0, f1)

    def wait_all(ref, sem):
        pltpu.make_async_copy(ref, ref, sem).wait()

    def send_faces(t):
        wait_all(r1[t].at[pl.ds(0, 7)], rsem.at[10 + t])

        def piece(key):
            pair = r1[t][(key & 15) >> 1]
            return jnp.where((key & 1) == 0, pair[0:8], pair[8:16])

        r2[t][me] = piece(my_key)

        def body(k, carry):
            to = far_first(k)
            p2[t, to] = piece(keys[0, to])
            remote(p2.at[t, to], r2[t].at[me], 12 + t, (region, to)).start()
            return carry

        lax.fori_loop(0, INNER - 1, body, 0)

    send_faces(0)
    send_faces(1)

    q4, z = lane // 32, lane % 32
    edge_y = jnp.where((lane < 32) & (sub == 0) | (lane >= 96) & (sub == 7), 1.0, 0.0)
    sign_y = jnp.where(lane < 64, edge_y, -edge_y)
    edge_z = jnp.where((z == 0) | (z == 31), 1.0, 0.0)
    sign_z = jnp.where(z < 16, edge_z, -edge_z)
    pick_x = (q4 // 2) * 16 + z // 2
    pick_z = (q4 // 2) * 2 + z // 16

    def add_ghosts(t, dst):
        wait_all(r2[t].at[pl.ds(0, INNER - 1)], rsem.at[12 + t])
        start = (my_key >> 4) * 8
        for k in range(8):
            gt[pl.ds(k * 8, 8)] = r2[t][start + k]
        tiles = [gt[pl.ds(face, 8, stride=8)] for face in range(6)]
        for face, x in ((0, 1), (1, 32)):
            e = [take(tiles[face], pick_x + 32 * v) for v in range(4)]
            dst[0, x] = dst[0, x] + e[0]
            dst[1, x] = dst[1, x] + e[0] if face == 0 else dst[1, x] - e[0]
            dst[2, x] = dst[2, x] + e[1]
            dst[3, x] = dst[3, x] + e[2]
            dst[4, x] = dst[4, x] + e[3]
        for v in range(4):
            for odd in range(2):
                pick = v * 32 + odd * 16 + z // 2
                ey[v, pl.ds(odd, 8, stride=2)] = jnp.where(lane < 64, take(tiles[2], pick), take(tiles[3], pick))

        def body(x, carry):
            y = [jnp.broadcast_to(ey[v, pl.ds(x, 1)], (8, 128)) for v in range(4)]
            zz = [take(tiles[4 + v // 2], pick_z + ((v % 2) * 64 + x * 4)) for v in range(4)]
            add = [
                edge_y * y[0] + edge_z * zz[0],
                edge_y * y[1] + edge_z * zz[1],
                sign_y * y[0] + edge_z * zz[2],
                edge_y * y[2] + sign_z * zz[0],
                edge_y * y[3] + edge_z * zz[3],
            ]
            for i in range(5):
                dst[i, 2 * x + 1] = dst[i, 2 * x + 1] + add[i]
                dst[i, 2 * x + 2] = dst[i, 2 * x + 2] + add[i]
            return carry

        lax.fori_loop(0, 16, body, 0)

    live = [jnp.where(turn < count, 1.0, 0.0) for turn in range(BURN_MAX)]
    group = 16

    def burn(dst):
        def body(g, carry):
            at = g * group
            p = [dst[0, at + i + 1] for i in range(group)]
            f = [dst[4, at + i + 1] for i in range(group)]
            for turn in range(BURN_MAX):
                for i in range(group):
                    r = pl.reciprocal(fa[at + i] + fb[at + i] * jnp.tanh(p[i]), approx=True)
                    d = live[turn] * (f[i] - f[i] * r)
                    f[i] = f[i] - d
                    p[i] = p[i] + 0.5 * d
            for i in range(group):
                dst[0, at + i + 1] = p[i]
                dst[4, at + i + 1] = f[i]
            return carry

        lax.fori_loop(0, 32 // group, body, 0)

    add_ghosts(0, f1)
    burn(f1)
    fine_hydro(f1, f0)
    add_ghosts(1, f0)
    burn(f0)

    stores = []
    for j in range(8):
        stores.append(
            pltpu.make_async_copy(
                f0.at[:, pl.ds(1, 32), j], fine_out.at[:, :, pl.ds(j * 128, 128)], lsem.at[2 + j]
            )
        )
        stores[-1].start()
    pick_m = ((lane % 32) // 16) * 64 + 2 * (lane % 16)

    def means(a, carry):
        for i in range(5):
            tile = zero
            for g in range(4):
                at = a * 8 + 2 * g
                q = f0[i, at + 1] + f0[i, at + 2]
                q = q + lanes(q, -1)
                q = q + lanes(q, -32)
                tile = jnp.where(q4 == g, take(q, pick_m), tile)
            mb[pl.ds(a * 64 + i, 8, stride=8)] = 0.125 * tile
        for i in range(5, 8):
            mb[pl.ds(a * 64 + i, 8, stride=8)] = zero
        return carry

    lax.fori_loop(0, 4, means, 0)

    r3[me] = mb[pl.ds(me * 8, 8)]

    def send_mean(k, carry):
        to = far_first(k)
        remote(mb.at[pl.ds(to * 8, 8)], r3.at[me], 14, (region, to)).start()
        return carry

    lax.fori_loop(0, INNER - 1, send_mean, 0)
    wait_all(r3.at[pl.ds(0, 31)], rsem.at[14])

    def pick_pair(to):
        return [r3[keys[1, 2 * to + s]] for s in range(2)]

    for s, q in enumerate(pick_pair(me)):
        r4[pl.ds(me * 16 + 8 * s, 8)] = q

    def send_pair(k, carry):
        to = far_first(k)
        for s, q in enumerate(pick_pair(to)):
            p4[pl.ds(to * 16 + 8 * s, 8)] = q
        remote(p4.at[pl.ds(to * 16, 16)], r4.at[pl.ds(me * 16, 16)], 15, (region, to)).start()
        return carry

    lax.fori_loop(0, INNER - 1, send_pair, 0)
    wait_all(r4.at[pl.ds(0, 31 * 16)], rsem.at[15])

    def place(n, carry):
        i, a = n // 4, n % 4
        for s in range(2):
            tile = r4[pl.ds(a * 128 + s * 8 + i, 8, stride=16)]
            here = lane // 16 == slots[s]
            for g in range(4):
                for odd in range(2):
                    at = pl.ds((a * 4 + g) * 16 + odd, 8, stride=2)
                    h[i, at] = jnp.where(here, take(tile, lane % 16 + (g * 32 + odd * 16)), h[i, at])
        return carry

    lax.fori_loop(0, 20, place, 0)
    last = pltpu.make_async_copy(h, coarse_out, lsem.at[0])
    last.start()

    for halo in halos:
        halo.wait_send()
    for t in range(2):
        wait_all(p1.at[t, pl.ds(0, 7 * 16)], ssem.at[10 + t])
        wait_all(p2.at[t, pl.ds(0, INNER - 1)], ssem.at[12 + t])
    wait_all(mb.at[pl.ds(0, 31 * 8)], ssem.at[14])
    wait_all(p4.at[pl.ds(0, 31 * 16)], ssem.at[15])
    for store in stores:
        store.wait()
    last.wait()


def per_device(coarse_state, fine_state, coarse_rate, fine_rate, parents, burn_steps):
    vmem, smem, anywhere = (
        pl.BlockSpec(memory_space=pltpu.VMEM),
        pl.BlockSpec(memory_space=pltpu.SMEM),
        pl.BlockSpec(memory_space=pl.ANY),
    )
    coarse_new, fine_new = pl.pallas_call(
        kernel,
        out_shape=(
            jax.ShapeDtypeStruct((5, 256, 128), F32),
            jax.ShapeDtypeStruct((5, 32, 1024), F32),
        ),
        in_specs=[anywhere, anywhere, anywhere, anywhere, vmem, smem],
        out_specs=(anywhere, anywhere),
        scratch_shapes=[
            pltpu.VMEM((5, 288, 128), F32),
            pltpu.VMEM((5, 256, 128), F32),
            pltpu.VMEM((256, 128), F32),
            pltpu.VMEM((2, 5, 32, 128), F32),
            pltpu.VMEM((2, 16, 128), F32),
            pltpu.VMEM((2, 11, 16, 128), F32),
            pltpu.VMEM((2, 11, 16, 128), F32),
            pltpu.VMEM((4, 8, 128), F32),
            pltpu.VMEM((4, 8, 128), F32),
            pltpu.VMEM((4, 4, 16, 128), F32),
            pltpu.VMEM((4, 256, 128), F32),
            pltpu.VMEM((8, 128), jnp.int32),
            pltpu.SMEM((8, 128), jnp.int32),
            pltpu.VMEM((2, 128, 128), F32),
            pltpu.VMEM((8, 16, 128), F32),
            pltpu.VMEM((8, 16, 128), F32),
            pltpu.VMEM((2, 32, 8, 128), F32),
            pltpu.VMEM((32, 8, 128), F32),
            pltpu.VMEM((32, 8, 128), F32),
            pltpu.VMEM((5, 34, 8, 128), F32),
            pltpu.VMEM((5, 34, 8, 128), F32),
            pltpu.VMEM((32, 8, 128), F32),
            pltpu.VMEM((32, 8, 128), F32),
            pltpu.VMEM((32, 8, 128), F32),
            pltpu.VMEM((64, 128), F32),
            pltpu.VMEM((4, 16, 128), F32),
            pltpu.VMEM((256, 128), F32),
            pltpu.VMEM((32, 8, 128), F32),
            pltpu.VMEM((512, 128), F32),
            pltpu.VMEM((512, 128), F32),
            pltpu.SemaphoreType.DMA((16,)),
            pltpu.SemaphoreType.DMA((16,)),
            pltpu.SemaphoreType.DMA((18,)),
            pltpu.SemaphoreType.DMA,
        ],
        compiler_params=pltpu.CompilerParams(
            collective_id=0, has_side_effects=True, vmem_limit_bytes=40 * 2**20
        ),
        name="reactive_step",
    )(
        coarse_state.reshape(5, 256, 128),
        fine_state.reshape(5, 32, 1024),
        coarse_rate.reshape(256, 128),
        fine_rate.reshape(32, 1024),
        parents,
        burn_steps,
    )
    return coarse_new.reshape(5, 16, 16, 128), fine_new.reshape(1, 5, 32, 1024)


def solution(mesh):
    in_specs = (
        P(None, "region", "inner", None),
        P(("region", "inner"), None, None, None),
        P("region", "inner", None),
        P(("region", "inner"), None, None),
        P("region", None),
        P(("region", "inner")),
    )
    out_specs = (P(None, "region", "inner", None), P(("region", "inner"), None, None, None))
    return jax.shard_map(per_device, mesh=mesh, in_specs=in_specs, out_specs=out_specs, check_vma=False)
```

profile of v0, /device:TPU:1, one launch (start us, length us, event | category | flops | bytes accessed | tf_op | source)
XLA Modules:
  0.0 55.6 jit_solution(1887797012601839613)
XLA Ops:
  1.3 0.0 copy-start.4
  1.3 0.6 %copy-done.4 = s32[1,32]{1,0:T(1,128)S(1)} copy-done((s32[1,32]{1,0:T(1,128)S(1)}, s32[1,32]{1,0:T(1,128)}, u32[]{:S(2)}) %copy-start.4) | copy-done | bytes 152
  1.9 0.0 copy-start
  1.9 1.1 %copy-done = f32[5,16,16,128]{3,2,1,0:T(8,128)S(1)} copy-done((f32[5,16,16,128]{3,2,1,0:T(8,128)S(1)}, f32[5,16,16,128]{3,2,1,0:T(8,128)}, u32[]{:S(2)}) %copy-start) | copy-done | bytes 655384
  3.0 0.0 copy-start.1
  3.0 1.1 %copy-done.1 = f32[1,5,32,1024]{3,2,1,0:T(8,128)S(1)} copy-done((f32[1,5,32,1024]{3,2,1,0:T(8,128)S(1)}, f32[1,5,32,1024]{3,2,1,0:T(8,128)}, u32[]{:S(2)}) %copy-start.1) | copy-done | bytes 655384
  4.1 0.0 copy-start.2
  4.1 0.9 %copy-done.2 = f32[16,16,128]{2,1,0:T(8,128)S(1)} copy-done((f32[16,16,128]{2,1,0:T(8,128)S(1)}, f32[16,16,128]{2,1,0:T(8,128)}, u32[]{:S(2)}) %copy-start.2) | copy-done | bytes 131096
  5.0 0.0 copy-start.3
  5.0 0.9 %copy-done.3 = f32[1,32,1024]{2,1,0:T(8,128)S(1)} copy-done((f32[1,32,1024]{2,1,0:T(8,128)S(1)}, f32[1,32,1024]{2,1,0:T(8,128)}, u32[]{:S(2)}) %copy-start.3) | copy-done | bytes 131096
  5.9 48.0 %reactive_step.1 = (f32[5,256,128]{2,1,0:T(8,128)S(1)}, f32[5,32,1024]{2,1,0:T(8,128)S(1)}) custom-call(f32[5,256,128]{2,1,0:T(8,128)S(1)} %bitcast.6, f32[5,32,1024]{2,1,0:T(8,128)S(1)} %bitcast.7, f32[256,128]{1,0:T(8,128)S(1)} %bitcast.10, f32[32,1024]{1,0:T(8,128)S(1)} %bitcast.11, s32[1,32]{1,0:T(1,128)S(1)} %copy-done.4, s32[1]{0:T(128)S(6)} %copy.10.steps), custom_call_target="tpu_custom_call" | custom-call | tf_op jit(solution)/shard_map/reactive_step/pallas_call | solution.py:605
  54.0 0.8 %copy.11 = f32[5,16,16,128]{3,2,1,0:T(8,128)} copy(f32[5,16,16,128]{3,2,1,0:T(8,128)S(1)} %bitcast.9) | data formatting | bytes 1310720
  54.8 0.8 %copy.12 = f32[1,5,32,1024]{3,2,1,0:T(8,128)} copy(f32[1,5,32,1024]{3,2,1,0:T(8,128)S(1)} %bitcast.8) | data formatting | bytes 1310720
Async XLA Ops:
  1.3 0.7 %copy-start.4 = (s32[1,32]{1,0:T(1,128)S(1)}, s32[1,32]{1,0:T(1,128)}, u32[]{:S(2)}) copy-start(s32[1,32]{1,0:T(1,128)} %parents.1) | copy-start | bytes 388
  1.9 1.1 %copy-start = (f32[5,16,16,128]{3,2,1,0:T(8,128)S(1)}, f32[5,16,16,128]{3,2,1,0:T(8,128)}, u32[]{:S(2)}) copy-start(f32[5,16,16,128]{3,2,1,0:T(8,128)} %param.6) | copy-start | bytes 1966084
  3.0 1.1 %copy-start.1 = (f32[1,5,32,1024]{3,2,1,0:T(8,128)S(1)}, f32[1,5,32,1024]{3,2,1,0:T(8,128)}, u32[]{:S(2)}) copy-start(f32[1,5,32,1024]{3,2,1,0:T(8,128)} %param.7) | copy-start | bytes 1966084
  4.1 0.9 %copy-start.2 = (f32[16,16,128]{2,1,0:T(8,128)S(1)}, f32[16,16,128]{2,1,0:T(8,128)}, u32[]{:S(2)}) copy-start(f32[16,16,128]{2,1,0:T(8,128)} %param.8) | copy-start | bytes 393220
  5.0 0.9 %copy-start.3 = (f32[1,32,1024]{2,1,0:T(8,128)S(1)}, f32[1,32,1024]{2,1,0:T(8,128)}, u32[]{:S(2)}) copy-start(f32[1,32,1024]{2,1,0:T(8,128)} %param.9) | copy-start | bytes 393220
where the time goes:
time: 55.9 us; the launch traced here: 55.6 us
  Pallas kernels  48 us (86%)
  local copies, waits for them, and re-layouts  6.3 us (11%)
  between operations  1.3 us (2%)
    pallas_call x1, Pallas kernels, per_device(): pl.pallas_call(kernel, out_shape=(jax.ShapeDtypeStruct((5, 256, 128), F32...  48 us
    unnamed x12, local copies, waits for them, and re-layouts  6.3 us

commit v1 on v0

--- a/solution.py
+++ b/solution.py
@@ -123,9 +123,9 @@
 
 
 def kernel(
-    coarse, fine, crate, frate, parents, steps, coarse_out, fine_out,
+    coarse, fine, crate, frate, parents, steps, h_out, fine_out, r4, table_out,
     c, h, cr, xh, xr, ys, yh, ds, dr, fv, zv, table, keys, p1, r1a, r1b, p2, r2a, r2b, f0, f1, fa, fb, fr, gt, ey,
-    mb, r3, p4, r4, ssem, rsem, lsem, tsem,
+    mb, r3, p4, pv, sv, ssem, rsem, lsem, tsem,
 ):
     r1, r2 = (r1a, r1b), (r2a, r2b)
     region, me = lax.axis_index("region"), lax.axis_index("inner")
@@ -134,9 +134,24 @@
     plane, mine = (me // 8) * 8, lax.rem(me, 8)
     sub, lane = iota((8, 128), 0), iota((8, 128), 1)
 
+    def far_first(k):
+        return lax.rem(me + 1 + lax.rem(15 + k, INNER - 1), INNER)
+
+    barrier = pltpu.get_barrier_semaphore()
+    others = [(up, right), (up, left), (down, right), (down, left), (up, me), (down, me)]
+    for other in others:
+        pl.semaphore_signal(barrier, inc=1, device_id=other, device_id_type=MESH)
+
+    def greet(k, carry):
+        pl.semaphore_signal(barrier, inc=1, device_id=(region, far_first(k)), device_id_type=MESH)
+        return carry
+
+    lax.fori_loop(0, INNER - 1, greet, 0)
     loads = [
         pltpu.make_async_copy(coarse, c.at[:, pl.ds(16, 256)], lsem.at[0]),
         pltpu.make_async_copy(crate, cr, lsem.at[1]),
+        pltpu.make_async_copy(parents, pv, lsem.at[18]),
+        pltpu.make_async_copy(steps, sv, lsem.at[19]),
     ]
     for j in range(8):
         cut = pl.ds(j * 128, 128)
@@ -144,41 +159,6 @@
         loads.append(pltpu.make_async_copy(frate.at[:, cut], fr.at[:, j], lsem.at[10 + j]))
     for load in loads:
         load.start()
-    barrier = pltpu.get_barrier_semaphore()
-
-    def greet(k, carry):
-        pl.semaphore_signal(
-            barrier, inc=1, device_id=(region, lax.rem(me + 1 + k, INNER)), device_id_type=MESH
-        )
-        return carry
-
-    lax.fori_loop(0, INNER - 1, greet, 0)
-    others = [(up, me), (down, me), (up, right), (up, left), (down, right), (down, left)]
-    for other in others:
-        pl.semaphore_signal(barrier, inc=1, device_id=other, device_id_type=MESH)
-
-    block_row = jnp.broadcast_to(parents[...], (32, 32))
-    ri, ci = iota((32, 32), 0), iota((32, 32), 1)
-    block = jnp.sum(jnp.where(ri == ci, block_row, 0), axis=1, keepdims=True)
-    owner = block >> 3
-    slot = jnp.sum(
-        jnp.where((jnp.broadcast_to(owner, (32, 32)) == (block_row >> 3)) & (ci < ri), 1, 0),
-        axis=1,
-        keepdims=True,
-    )
-    key = jnp.broadcast_to(owner * 2 + slot, (32, 128))
-    ri, ci = iota((32, 128), 0), iota((32, 128), 1)
-    layer = jnp.broadcast_to((block & 7) + 1, (32, 128))
-    key_row = jnp.sum(jnp.where(ri == ci, key, 0), axis=0, keepdims=True)
-    patch_row = jnp.sum(jnp.where(key == ci, ri, 0), axis=0, keepdims=True)
-    layer_row = jnp.sum(jnp.where(key == ci, layer, 0), axis=0, keepdims=True) - 1
-    table[...] = jnp.where(
-        sub == 0,
-        jnp.broadcast_to(key_row, (8, 128)),
-        jnp.where(sub == 1, jnp.broadcast_to(patch_row, (8, 128)), jnp.broadcast_to(layer_row, (8, 128))),
-    )
-    look = pltpu.make_async_copy(table, keys, tsem)
-    look.start()
 
     zero = jnp.zeros((8, 128), F32)
     for i in range(5):
@@ -223,6 +203,32 @@
     for halo in halos:
         halo.start()
 
+    loads[2].wait()
+    block_row = jnp.broadcast_to(pv[...], (32, 32))
+    ri, ci = iota((32, 32), 0), iota((32, 32), 1)
+    block = jnp.sum(jnp.where(ri == ci, block_row, 0), axis=1, keepdims=True)
+    owner = block >> 3
+    slot = jnp.sum(
+        jnp.where((jnp.broadcast_to(owner, (32, 32)) == (block_row >> 3)) & (ci < ri), 1, 0),
+        axis=1,
+        keepdims=True,
+    )
+    key = jnp.broadcast_to(owner * 2 + slot, (32, 128))
+    ri, ci = iota((32, 128), 0), iota((32, 128), 1)
+    layer = jnp.broadcast_to((block & 7) + 1, (32, 128))
+    key_row = jnp.sum(jnp.where(ri == ci, key, 0), axis=0, keepdims=True)
+    patch_row = jnp.sum(jnp.where(key == ci, ri, 0), axis=0, keepdims=True)
+    layer_row = jnp.sum(jnp.where(key == ci, layer, 0), axis=0, keepdims=True) - 1
+    table[...] = jnp.where(
+        sub == 0,
+        jnp.broadcast_to(key_row, (8, 128)),
+        jnp.where(sub == 1, jnp.broadcast_to(patch_row, (8, 128)), jnp.broadcast_to(layer_row, (8, 128))),
+    )
+    keep = pltpu.make_async_copy(table, table_out, lsem.at[18])
+    keep.start()
+    look = pltpu.make_async_copy(table, keys, tsem)
+    look.start()
+
     shifts = coarse_shifts((16, 128))
 
     def coarse_plane(x, carry):
@@ -234,7 +240,7 @@
             h[i, pl.ds(at, 16)] = q
         return carry
 
-    lax.fori_loop(0, 16, coarse_plane, 0)
+    lax.fori_loop(0, 16, coarse_plane, 0, unroll=4)
 
     look.wait()
     slots = [keys[2, 2 * me], keys[2, 2 * me + 1]]
@@ -260,7 +266,7 @@
             zv[3, pl.ds(at, 16)] = f * jnp.where(low, NB * (1 + ADV[2]), NB * (1 - ADV[2]))
             return carry
 
-        lax.fori_loop(0, 16, body, 0)
+        lax.fori_loop(0, 16, body, 0, unroll=4)
 
     def z_tiles():
         def body(x, tiles):
@@ -273,7 +279,7 @@
                         tiles[s * 2 + v // 2] = jnp.where(here, take(q, picks[s]), tiles[s * 2 + v // 2])
             return tuple(tiles)
 
-        tiles = lax.fori_loop(0, 16, body, (zero,) * 4)
+        tiles = lax.fori_loop(0, 16, body, (zero,) * 4, unroll=8)
         return [[tiles[s * 2 + w] * inside[s] for w in range(2)] for s in range(2)]
 
     def xy_tile(face, s):
@@ -286,15 +292,10 @@
         return tile
 
     def put_tile(t, s, face, tile):
-        p1[t, pl.ds(s * 8 + face, 8, stride=16)] = tile
+        p1[t, pl.ds(s * 6 + face, 8, stride=16)] = tile
 
     def get_tile(t, s, face):
-        return p1[t, pl.ds(s * 8 + face, 8, stride=16)]
-
-    for t in range(2):
-        for s in range(2):
-            for face in (6, 7):
-                put_tile(t, s, face, zero)
+        return p1[t, pl.ds(s * 6 + face, 8, stride=16)]
 
     z_values(c, 16)
     for s, pair in enumerate(z_tiles()):
@@ -324,19 +325,16 @@
             put_tile(0, s, face, xy_tile(face, s))
 
     def send_pieces(t):
-        r1[t][mine] = p1[t, pl.ds(mine * 16, 16)]
+        r1[t][mine, 0:12] = p1[t, pl.ds(mine * 16, 12)]
 
         def body(k, carry):
             to = lax.rem(mine + 1 + k, 8)
             remote(
-                p1.at[t, pl.ds(to * 16, 16)], r1[t].at[mine], 10 + t, (region, plane + to)
+                p1.at[t, pl.ds(to * 16, 12)], r1[t].at[mine, pl.ds(0, 12)], 10 + t, (region, plane + to)
             ).start()
             return carry
 
         lax.fori_loop(0, 7, body, 0)
-
-    def far_first(k):
-        return lax.rem(me + 1 + lax.rem(15 + k, INNER - 1), INNER)
 
     send_pieces(0)
 
@@ -362,7 +360,7 @@
         h[4, pl.ds(at, 64)] = f
         return carry
 
-    lax.fori_loop(0, 4, coarse_burn, 0)
+    lax.fori_loop(0, 4, coarse_burn, 0, unroll=4)
 
     def own_rows(axis, e):
         if axis == 0:
@@ -395,10 +393,12 @@
         for face in range(4):
             put_tile(1, s, face, 0.5 * (get_tile(0, s, face) + xy_tile(face, s)))
     send_pieces(1)
-
-    for load in loads[2:]:
+    stores = [pltpu.make_async_copy(h, h_out, lsem.at[0])]
+    stores[0].start()
+
+    for load in loads[3:]:
         load.wait()
-    count = steps[0]
+    count = sv[0]
     counted = jnp.broadcast_to(count, (8, 128)).astype(F32)
     span = 0.25 / counted
     fine_shift = fine_shifts()
@@ -409,7 +409,7 @@
         fb[x] = 0.5 * q
         return carry
 
-    lax.fori_loop(0, 32, rates, 0)
+    lax.fori_loop(0, 32, rates, 0, unroll=8)
 
     def fine_hydro(src, dst):
         def body(x, carry):
@@ -420,7 +420,7 @@
                 dst[i, x + 1] = q
             return carry
 
-        lax.fori_loop(0, 32, body, 0)
+        lax.fori_loop(0, 32, body, 0, unroll=8)
 
     fine_hydro(f0, f1)
 
@@ -428,18 +428,18 @@
         pltpu.make_async_copy(ref, ref, sem).wait()
 
     def send_faces(t):
-        wait_all(r1[t].at[pl.ds(0, 7)], rsem.at[10 + t])
+        wait_all(r1[t].at[pl.ds(0, 7), pl.ds(0, 12)], rsem.at[10 + t])
 
         def piece(key):
             pair = r1[t][(key & 15) >> 1]
-            return jnp.where((key & 1) == 0, pair[0:8], pair[8:16])
-
-        r2[t][me] = piece(my_key)
+            return jnp.where((key & 1) == 0, pair[0:6], pair[6:12])
+
+        r2[t][me, 0:6] = piece(my_key)
 
         def body(k, carry):
             to = far_first(k)
-            p2[t, to] = piece(keys[0, to])
-            remote(p2.at[t, to], r2[t].at[me], 12 + t, (region, to)).start()
+            p2[t, to, 0:6] = piece(keys[0, to])
+            remote(p2.at[t, to, pl.ds(0, 6)], r2[t].at[me, pl.ds(0, 6)], 12 + t, (region, to)).start()
             return carry
 
         lax.fori_loop(0, INNER - 1, body, 0)
@@ -456,7 +456,7 @@
     pick_z = (q4 // 2) * 2 + z // 16
 
     def add_ghosts(t, dst):
-        wait_all(r2[t].at[pl.ds(0, INNER - 1)], rsem.at[12 + t])
+        wait_all(r2[t].at[pl.ds(0, INNER - 1), pl.ds(0, 6)], rsem.at[12 + t])
         start = (my_key >> 4) * 8
         for k in range(8):
             gt[pl.ds(k * 8, 8)] = r2[t][start + k]
@@ -488,7 +488,7 @@
                 dst[i, 2 * x + 2] = dst[i, 2 * x + 2] + add[i]
             return carry
 
-        lax.fori_loop(0, 16, body, 0)
+        lax.fori_loop(0, 16, body, 0, unroll=8)
 
     live = [jnp.where(turn < count, 1.0, 0.0) for turn in range(BURN_MAX)]
     group = 16
@@ -517,7 +517,6 @@
     add_ghosts(1, f0)
     burn(f0)
 
-    stores = []
     for j in range(8):
         stores.append(
             pltpu.make_async_copy(
@@ -537,79 +536,100 @@
                 q = q + lanes(q, -32)
                 tile = jnp.where(q4 == g, take(q, pick_m), tile)
             mb[pl.ds(a * 64 + i, 8, stride=8)] = 0.125 * tile
-        for i in range(5, 8):
-            mb[pl.ds(a * 64 + i, 8, stride=8)] = zero
         return carry
 
-    lax.fori_loop(0, 4, means, 0)
-
-    r3[me] = mb[pl.ds(me * 8, 8)]
+    lax.fori_loop(0, 4, means, 0, unroll=2)
+
+    r3[me, 0:5] = mb[pl.ds(me * 8, 5)]
 
     def send_mean(k, carry):
         to = far_first(k)
-        remote(mb.at[pl.ds(to * 8, 8)], r3.at[me], 14, (region, to)).start()
+        remote(mb.at[pl.ds(to * 8, 5)], r3.at[me, pl.ds(0, 5)], 14, (region, to)).start()
         return carry
 
     lax.fori_loop(0, INNER - 1, send_mean, 0)
-    wait_all(r3.at[pl.ds(0, 31)], rsem.at[14])
+    wait_all(r3.at[pl.ds(0, 31), pl.ds(0, 5)], rsem.at[14])
 
     def pick_pair(to):
-        return [r3[keys[1, 2 * to + s]] for s in range(2)]
-
-    for s, q in enumerate(pick_pair(me)):
-        r4[pl.ds(me * 16 + 8 * s, 8)] = q
+        for s in range(2):
+            p4[to, 5 * s : 5 * s + 5] = r3[keys[1, 2 * to + s], 0:5]
+
+    pick_pair(me)
+    stores.append(pltpu.make_async_copy(p4.at[me], r4.at[me], lsem.at[1]))
+    stores[-1].start()
 
     def send_pair(k, carry):
         to = far_first(k)
-        for s, q in enumerate(pick_pair(to)):
-            p4[pl.ds(to * 16 + 8 * s, 8)] = q
-        remote(p4.at[pl.ds(to * 16, 16)], r4.at[pl.ds(me * 16, 16)], 15, (region, to)).start()
+        pick_pair(to)
+        remote(p4.at[to], r4.at[me], 15, (region, to)).start()
         return carry
 
     lax.fori_loop(0, INNER - 1, send_pair, 0)
-    wait_all(r4.at[pl.ds(0, 31 * 16)], rsem.at[15])
-
-    def place(n, carry):
-        i, a = n // 4, n % 4
-        for s in range(2):
-            tile = r4[pl.ds(a * 128 + s * 8 + i, 8, stride=16)]
-            here = lane // 16 == slots[s]
+
+    for halo in halos:
+        halo.wait_send()
+    for t in range(2):
+        wait_all(r1[t].at[pl.ds(0, 7), pl.ds(0, 12)], ssem.at[10 + t])
+        wait_all(r2[t].at[pl.ds(0, INNER - 1), pl.ds(0, 6)], ssem.at[12 + t])
+    wait_all(r3.at[pl.ds(0, 31), pl.ds(0, 5)], ssem.at[14])
+    wait_all(p4.at[pl.ds(0, 31)], ssem.at[15])
+    for store in stores:
+        store.wait()
+    keep.wait()
+    wait_all(r4.at[pl.ds(0, 31)], rsem.at[15])
+
+
+def place(stepped, means, fine, table, coarse_out, fine_out, h, m, f, keys, sem):
+    me = lax.axis_index("inner")
+    loads = [
+        pltpu.make_async_copy(means, m.at[:, pl.ds(0, 10)], sem.at[0]),
+        pltpu.make_async_copy(table, keys, sem.at[1]),
+        pltpu.make_async_copy(stepped, h, sem.at[2]),
+    ]
+    move = pltpu.make_async_copy(fine, f, sem.at[3])
+    for load in loads:
+        load.start()
+    move.start()
+    for load in loads:
+        load.wait()
+    lane = iota((8, 128), 1)
+    here = [lane // 16 == keys[2, 2 * me + s] for s in range(2)]
+    rows_of = m.reshape(512, 128)
+    move.wait()
+    stores = [pltpu.make_async_copy(f, fine_out, sem.at[3])]
+    stores[0].start()
+    for i in range(5):
+
+        def body(a, carry):
+            tiles = [rows_of[pl.ds(a * 128 + s * 5 + i, 8, stride=16)] for s in range(2)]
             for g in range(4):
                 for odd in range(2):
                     at = pl.ds((a * 4 + g) * 16 + odd, 8, stride=2)
-                    h[i, at] = jnp.where(here, take(tile, lane % 16 + (g * 32 + odd * 16)), h[i, at])
-        return carry
-
-    lax.fori_loop(0, 20, place, 0)
-    last = pltpu.make_async_copy(h, coarse_out, lsem.at[0])
-    last.start()
-
-    for halo in halos:
-        halo.wait_send()
-    for t in range(2):
-        wait_all(p1.at[t, pl.ds(0, 7 * 16)], ssem.at[10 + t])
-        wait_all(p2.at[t, pl.ds(0, INNER - 1)], ssem.at[12 + t])
-    wait_all(mb.at[pl.ds(0, 31 * 8)], ssem.at[14])
-    wait_all(p4.at[pl.ds(0, 31 * 16)], ssem.at[15])
+                    q = h[i, at]
+                    for s in range(2):
+                        q = jnp.where(here[s], take(tiles[s], lane % 16 + (g * 32 + odd * 16)), q)
+                    h[i, at] = q
+            return carry
+
+        lax.fori_loop(0, 4, body, 0, unroll=4)
+        stores.append(pltpu.make_async_copy(h.at[i], coarse_out.at[i], sem.at[4 + i]))
+        stores[-1].start()
     for store in stores:
         store.wait()
-    last.wait()
 
 
 def per_device(coarse_state, fine_state, coarse_rate, fine_rate, parents, burn_steps):
-    vmem, smem, anywhere = (
-        pl.BlockSpec(memory_space=pltpu.VMEM),
-        pl.BlockSpec(memory_space=pltpu.SMEM),
-        pl.BlockSpec(memory_space=pl.ANY),
-    )
-    coarse_new, fine_new = pl.pallas_call(
+    anywhere = pl.BlockSpec(memory_space=pl.ANY)
+    stepped, fine_mid, means, table = pl.pallas_call(
         kernel,
         out_shape=(
             jax.ShapeDtypeStruct((5, 256, 128), F32),
             jax.ShapeDtypeStruct((5, 32, 1024), F32),
+            jax.ShapeDtypeStruct((32, 10, 128), F32),
+            jax.ShapeDtypeStruct((8, 128), jnp.int32),
         ),
-        in_specs=[anywhere, anywhere, anywhere, anywhere, vmem, smem],
-        out_specs=(anywhere, anywhere),
+        in_specs=[anywhere] * 6,
+        out_specs=(anywhere,) * 4,
         scratch_shapes=[
             pltpu.VMEM((5, 288, 128), F32),
             pltpu.VMEM((5, 256, 128), F32),
@@ -639,15 +659,16 @@
             pltpu.VMEM((4, 16, 128), F32),
             pltpu.VMEM((256, 128), F32),
             pltpu.VMEM((32, 8, 128), F32),
-            pltpu.VMEM((512, 128), F32),
-            pltpu.VMEM((512, 128), F32),
+            pltpu.VMEM((32, 10, 128), F32),
+            pltpu.VMEM((1, 32), jnp.int32),
+            pltpu.SMEM((1,), jnp.int32),
             pltpu.SemaphoreType.DMA((16,)),
             pltpu.SemaphoreType.DMA((16,)),
-            pltpu.SemaphoreType.DMA((18,)),
+            pltpu.SemaphoreType.DMA((20,)),
             pltpu.SemaphoreType.DMA,
         ],
         compiler_params=pltpu.CompilerParams(
-            collective_id=0, has_side_effects=True, vmem_limit_bytes=40 * 2**20
+            collective_id=0, has_side_effects=True, vmem_limit_bytes=60 * 2**20
         ),
         name="reactive_step",
     )(
@@ -658,6 +679,24 @@
         parents,
         burn_steps,
     )
+    coarse_new, fine_new = pl.pallas_call(
+        place,
+        out_shape=(
+            jax.ShapeDtypeStruct((5, 256, 128), F32),
+            jax.ShapeDtypeStruct((5, 32, 1024), F32),
+        ),
+        in_specs=[anywhere] * 4,
+        out_specs=(anywhere,) * 2,
+        scratch_shapes=[
+            pltpu.VMEM((5, 256, 128), F32),
+            pltpu.VMEM((32, 16, 128), F32),
+            pltpu.VMEM((5, 32, 1024), F32),
+            pltpu.SMEM((8, 128), jnp.int32),
+            pltpu.SemaphoreType.DMA((9,)),
+        ],
+        compiler_params=pltpu.CompilerParams(vmem_limit_bytes=60 * 2**20),
+        name="place",
+    )(stepped, means, fine_mid, table)
     return coarse_new.reshape(5, 16, 16, 128), fine_new.reshape(1, 5, 32, 1024)
 
 

time: 55.9 us -> 42.3 us (0.76)
  Pallas kernels: 48 us -> 40.9 us
  local copies, waits for them, and re-layouts: 6.3 us -> 0 us
    pallas_call x1, Pallas kernels: 48 us -> 37.9 us  [per_device(): pl.pallas_call(kernel, out_shape=(jax.ShapeDtypeStruct((5, 256, 128), F32...]
    unnamed x12 -> x0, local copies, waits for them, and re-layouts: 6.3 us -> none
    pallas_call x0 -> x1, Pallas kernels: none -> 2.97 us  [per_device(): pl.pallas_call(place, out_shape=(jax.ShapeDtypeStruct((5, 256, 128), F32)...]
where the time goes in v1:
time: 42.3 us; the launch traced here: 42.1 us
  Pallas kernels  40.9 us (97%)
  between operations  1.29 us (3%)
    pallas_call x1, Pallas kernels, per_device(): pl.pallas_call(kernel, out_shape=(jax.ShapeDtypeStruct((5, 256, 128), F32...  37.9 us
    pallas_call x1, Pallas kernels, per_device(): pl.pallas_call(place, out_shape=(jax.ShapeDtypeStruct((5, 256, 128), F32)...  2.97 us

profile of v1, /device:TPU:1, one launch (start us, length us, event | category | flops | bytes accessed | tf_op | source)
XLA Modules:
  0.0 42.1 jit_solution(4662384613801632988)
XLA Ops:
  1.3 37.9 %reactive_step.1 = (f32[5,256,128]{2,1,0:T(8,128)}, f32[5,32,1024]{2,1,0:T(8,128)}, f32[32,10,128]{2,1,0:T(8,128)}, s32[8,128]{1,0:T(8,128)}) custom-call(f32[5,256,128]{2,1,0:T(8,128)} %bitcast.6, f32[5,32,1024]{2,1,0:T(8,128)} %bitcast.7, f32[256,128]{1,0:T(8,128)} %bitcast.8, f32[32,1024]{1,0:T(8,128)} %bitcast.9, s32[1,32]{1,0:T(1,128)} %parents.1, ...), custom_call_target="tpu_custom_call" | custom-call | tf_op jit(solution)/shard_map/reactive_step/pallas_call | solution.py:623
  39.2 3.0 %place.1 = (f32[5,256,128]{2,1,0:T(8,128)}, f32[5,32,1024]{2,1,0:T(8,128)}) custom-call(f32[5,256,128]{2,1,0:T(8,128)} %get-tuple-element.8.stepped, f32[32,10,128]{2,1,0:T(8,128)} %get-tuple-element.9.means, f32[5,32,1024]{2,1,0:T(8,128)} %get-tuple-element.10.fine, s32[8,128]{1,0:T(8,128)} %get-tuple-element.11.table), custom_call_target="tpu_custom_call" | custom-call | tf_op jit(solution)/shard_map/place/pallas_call | solution.py:682

commit v2 on v1

--- a/solution.py
+++ b/solution.py
@@ -125,7 +125,7 @@
 def kernel(
     coarse, fine, crate, frate, parents, steps, h_out, fine_out, r4, table_out,
     c, h, cr, xh, xr, ys, yh, ds, dr, fv, zv, table, keys, p1, r1a, r1b, p2, r2a, r2b, f0, f1, fa, fb, fr, gt, ey,
-    mb, r3, p4, pv, sv, ssem, rsem, lsem, tsem,
+    mb, r3, p4, pv, sv, ssem, rsem, lsem, tsem, ready,
 ):
     r1, r2 = (r1a, r1b), (r2a, r2b)
     region, me = lax.axis_index("region"), lax.axis_index("inner")
@@ -139,14 +139,20 @@
 
     barrier = pltpu.get_barrier_semaphore()
     others = [(up, right), (up, left), (down, right), (down, left), (up, me), (down, me)]
-    for other in others:
+    columns = [(region, lax.rem(me + 8 * k, INNER)) for k in (2, 1, 3)]
+    outside = [jnp.where(mine == 7, 1, 0), jnp.where(mine == 0, 1, 0)]
+    for other in others + columns:
         pl.semaphore_signal(barrier, inc=1, device_id=other, device_id_type=MESH)
-
-    def greet(k, carry):
-        pl.semaphore_signal(barrier, inc=1, device_id=(region, far_first(k)), device_id_type=MESH)
-        return carry
-
-    lax.fori_loop(0, INNER - 1, greet, 0)
+    for k in range(1, 8):
+        pl.semaphore_signal(
+            barrier, inc=1, device_id=(region, plane + lax.rem(mine + k, 8)), device_id_type=MESH
+        )
+    for e, other in enumerate((right, left)):
+
+        @pl.when(outside[e] == 1)
+        def _():
+            pl.semaphore_signal(barrier, inc=1, device_id=(region, other), device_id_type=MESH)
+
     loads = [
         pltpu.make_async_copy(coarse, c.at[:, pl.ds(16, 256)], lsem.at[0]),
         pltpu.make_async_copy(crate, cr, lsem.at[1]),
@@ -173,35 +179,43 @@
         for half in range(2):
             dst = pl.ds(half * 8, 8)
             for i in range(5):
-                ys[side, i, dst] = c[i, pl.ds(16 + half * 128 + near, 8, stride=16)]
-                ys[side, 6 + i, dst] = c[i, pl.ds(16 + half * 128 + far, 8, stride=16)]
-            ys[side, 5, dst] = cr[pl.ds(half * 128 + near, 8, stride=16)]
+                ys[side, 0, i, dst] = c[i, pl.ds(16 + half * 128 + near, 8, stride=16)]
+                ys[side, 1, i, dst] = c[i, pl.ds(16 + half * 128 + far, 8, stride=16)]
+            ys[side, 1, 5, dst] = cr[pl.ds(half * 128 + near, 8, stride=16)]
     for n, at in enumerate((255, 240, 15, 0)):
         for i in range(5):
             ds[n, i : i + 1] = c[i, 16 + at : 17 + at]
         ds[n, 5:8] = jnp.zeros((3, 128), F32)
 
-    pl.semaphore_wait(barrier, INNER - 1 + len(others))
+    pl.semaphore_wait(barrier, len(others) + len(columns) + 7 + outside[0] + outside[1])
 
     def remote(src, dst, n, to):
         return pltpu.make_async_remote_copy(
             src_ref=src, dst_ref=dst, send_sem=ssem.at[n], recv_sem=rsem.at[n], device_id=to, device_id_type=MESH
         )
 
-    halos = [
-        remote(ds.at[0], dr.at[0], 0, (up, right)),
-        remote(ds.at[1], dr.at[1], 1, (up, left)),
-        remote(ds.at[2], dr.at[2], 2, (down, right)),
-        remote(ds.at[3], dr.at[3], 3, (down, left)),
-        remote(ys.at[0], yh.at[0], 4, (region, right)),
-        remote(ys.at[1], yh.at[1], 5, (region, left)),
-        remote(c.at[:, pl.ds(16 + 224, 32)], xh.at[0], 6, (up, me)),
-        remote(c.at[:, pl.ds(16, 32)], xh.at[1], 7, (down, me)),
+    near = [
+        remote(c.at[:, pl.ds(16 + 240, 16)], xh.at[0, 0], 0, (up, me)),
+        remote(c.at[:, pl.ds(16, 16)], xh.at[1, 0], 1, (down, me)),
+        remote(ys.at[0, 0, pl.ds(0, 5)], yh.at[0, 0, pl.ds(0, 5)], 2, (region, right)),
+        remote(ys.at[1, 0, pl.ds(0, 5)], yh.at[1, 0, pl.ds(0, 5)], 3, (region, left)),
+    ]
+    far = [
+        remote(ds.at[0], dr.at[0], 4, (up, right)),
+        remote(ds.at[1], dr.at[1], 5, (up, left)),
+        remote(ds.at[2], dr.at[2], 6, (down, right)),
+        remote(ds.at[3], dr.at[3], 7, (down, left)),
         remote(cr.at[pl.ds(240, 16)], xr.at[0], 8, (up, me)),
         remote(cr.at[pl.ds(0, 16)], xr.at[1], 9, (down, me)),
+        remote(c.at[:, pl.ds(16 + 224, 16)], xh.at[0, 1], 16, (up, me)),
+        remote(c.at[:, pl.ds(32, 16)], xh.at[1, 1], 17, (down, me)),
+        remote(ys.at[0, 1], yh.at[0, 1], 18, (region, right)),
+        remote(ys.at[1, 1], yh.at[1, 1], 19, (region, left)),
     ]
-    for halo in halos:
+    for halo in near + far:
         halo.start()
+    for other in columns:
+        pl.semaphore_signal(ready, inc=1, device_id=other, device_id_type=MESH)
 
     loads[2].wait()
     block_row = jnp.broadcast_to(pv[...], (32, 32))
@@ -302,16 +316,16 @@
         for w, tile in enumerate(pair):
             put_tile(0, s, 4 + w, tile)
 
-    for halo in halos:
+    for halo in near:
         halo.wait_recv()
     mx = [jnp.where(region > 0, 1.0, 0.0), jnp.where(region < REGIONS - 1, 1.0, 0.0)]
     my = [jnp.where(me > 0, 1.0, 0.0), jnp.where(me < INNER - 1, 1.0, 0.0)]
 
     def near_x(e):
-        return [xh[e, i, pl.ds(16 - 16 * e, 16)] for i in range(5)]
+        return [xh[e, 0, i] for i in range(5)]
 
     def near_y(e):
-        return [yh[e, i] for i in range(5)]
+        return [yh[e, 0, i] for i in range(5)]
 
     for e in range(2):
         p, u, v, w, f = near_x(e)
@@ -362,6 +376,9 @@
 
     lax.fori_loop(0, 4, coarse_burn, 0, unroll=4)
 
+    for halo in far:
+        halo.wait_recv()
+
     def own_rows(axis, e):
         if axis == 0:
             return [c[i, pl.ds(16 + 240 * e, 16)] for i in range(5)]
@@ -374,15 +391,14 @@
         return [dr[n, i : i + 1] * scale for i in range(5)]
 
     for e in range(2):
-        far = [xh[e, i, pl.ds(16 * e, 16)] for i in range(5)]
         values = ghost_step(
-            near_x(e), far, own_rows(0, e), corner(2 * e, my[0]), corner(2 * e + 1, my[1]), xr[e], 0, e == 1
+            near_x(e), [xh[e, 1, i] for i in range(5)], own_rows(0, e), corner(2 * e, my[0]), corner(2 * e + 1, my[1]), xr[e], 0, e == 1
         )
         for i, q in enumerate(values):
             fv[e, i] = mx[e] * q
-        far = [yh[e, 6 + i] for i in range(5)]
         values = ghost_step(
-            near_y(e), far, own_rows(1, e), corner(e, mx[0]), corner(2 + e, mx[1]), yh[e, 5], 1, e == 1
+            near_y(e), [yh[e, 1, i] for i in range(5)], own_rows(1, e),
+            corner(e, mx[0]), corner(2 + e, mx[1]), yh[e, 1, 5], 1, e == 1,
         )
         for i, q in enumerate(values):
             fv[2 + e, i] = my[e] * q
@@ -444,6 +460,7 @@
 
         lax.fori_loop(0, INNER - 1, body, 0)
 
+    pl.semaphore_wait(ready, len(columns))
     send_faces(0)
     send_faces(1)
 
@@ -566,7 +583,7 @@
 
     lax.fori_loop(0, INNER - 1, send_pair, 0)
 
-    for halo in halos:
+    for halo in near + far:
         halo.wait_send()
     for t in range(2):
         wait_all(r1[t].at[pl.ds(0, 7), pl.ds(0, 12)], ssem.at[10 + t])
@@ -595,9 +612,7 @@
     lane = iota((8, 128), 1)
     here = [lane // 16 == keys[2, 2 * me + s] for s in range(2)]
     rows_of = m.reshape(512, 128)
-    move.wait()
-    stores = [pltpu.make_async_copy(f, fine_out, sem.at[3])]
-    stores[0].start()
+    stores = []
     for i in range(5):
 
         def body(a, carry):
@@ -614,6 +629,10 @@
         lax.fori_loop(0, 4, body, 0, unroll=4)
         stores.append(pltpu.make_async_copy(h.at[i], coarse_out.at[i], sem.at[4 + i]))
         stores[-1].start()
+        if i == 0:
+            move.wait()
+            stores.append(pltpu.make_async_copy(f, fine_out, sem.at[3]))
+            stores[-1].start()
     for store in stores:
         store.wait()
 
@@ -634,10 +653,10 @@
             pltpu.VMEM((5, 288, 128), F32),
             pltpu.VMEM((5, 256, 128), F32),
             pltpu.VMEM((256, 128), F32),
-            pltpu.VMEM((2, 5, 32, 128), F32),
+            pltpu.VMEM((2, 2, 5, 16, 128), F32),
             pltpu.VMEM((2, 16, 128), F32),
-            pltpu.VMEM((2, 11, 16, 128), F32),
-            pltpu.VMEM((2, 11, 16, 128), F32),
+            pltpu.VMEM((2, 2, 6, 16, 128), F32),
+            pltpu.VMEM((2, 2, 6, 16, 128), F32),
             pltpu.VMEM((4, 8, 128), F32),
             pltpu.VMEM((4, 8, 128), F32),
             pltpu.VMEM((4, 4, 16, 128), F32),
@@ -662,10 +681,11 @@
             pltpu.VMEM((32, 10, 128), F32),
             pltpu.VMEM((1, 32), jnp.int32),
             pltpu.SMEM((1,), jnp.int32),
-            pltpu.SemaphoreType.DMA((16,)),
-            pltpu.SemaphoreType.DMA((16,)),
+            pltpu.SemaphoreType.DMA((20,)),
+            pltpu.SemaphoreType.DMA((20,)),
             pltpu.SemaphoreType.DMA((20,)),
             pltpu.SemaphoreType.DMA,
+            pltpu.SemaphoreType.REGULAR,
         ],
         compiler_params=pltpu.CompilerParams(
             collective_id=0, has_side_effects=True, vmem_limit_bytes=60 * 2**20

time: 42.3 us -> 40.5 us (0.957)
  Pallas kernels: 40.9 us -> 39.1 us
    pallas_call x1, Pallas kernels: 37.9 us -> 36.2 us  [per_device(): pl.pallas_call(kernel, out_shape=(jax.ShapeDtypeStruct((5, 256, 128), F32...]
where the time goes in v2:
time: 40.5 us; the launch traced here: 40.4 us
  Pallas kernels  39.1 us (97%)
  between operations  1.29 us (3%)
    pallas_call x1, Pallas kernels, per_device(): pl.pallas_call(kernel, out_shape=(jax.ShapeDtypeStruct((5, 256, 128), F32...  36.2 us
    pallas_call x1, Pallas kernels, per_device(): pl.pallas_call(place, out_shape=(jax.ShapeDtypeStruct((5, 256, 128), F32)...  2.85 us

profile of v2, /device:TPU:1, one launch (start us, length us, event | category | flops | bytes accessed | tf_op | source)
XLA Modules:
  0.0 40.4 jit_solution(13606153625446493714)
XLA Ops:
  1.3 36.2 %reactive_step.1 = (f32[5,256,128]{2,1,0:T(8,128)}, f32[5,32,1024]{2,1,0:T(8,128)}, f32[32,10,128]{2,1,0:T(8,128)}, s32[8,128]{1,0:T(8,128)}) custom-call(f32[5,256,128]{2,1,0:T(8,128)} %bitcast.6, f32[5,32,1024]{2,1,0:T(8,128)} %bitcast.7, f32[256,128]{1,0:T(8,128)} %bitcast.8, f32[32,1024]{1,0:T(8,128)} %bitcast.9, s32[1,32]{1,0:T(1,128)} %parents.1, ...), custom_call_target="tpu_custom_call" | custom-call | tf_op jit(solution)/shard_map/reactive_step/pallas_call | solution.py:642
  37.5 2.8 %place.1 = (f32[5,256,128]{2,1,0:T(8,128)}, f32[5,32,1024]{2,1,0:T(8,128)}) custom-call(f32[5,256,128]{2,1,0:T(8,128)} %get-tuple-element.8.stepped, f32[32,10,128]{2,1,0:T(8,128)} %get-tuple-element.9.means, f32[5,32,1024]{2,1,0:T(8,128)} %get-tuple-element.10.fine, s32[8,128]{1,0:T(8,128)} %get-tuple-element.11.table), custom_call_target="tpu_custom_call" | custom-call | tf_op jit(solution)/shard_map/place/pallas_call | solution.py:702

commit v3 on v2

--- a/solution.py
+++ b/solution.py
@@ -15,6 +15,14 @@
 BURN_MAX = 8
 REGIONS = 4
 INNER = 32
+
+
+def hops(offset):
+    z, y = offset // 8, offset // 2 % 4
+    return min(z, 4 - z) + min(y, 4 - y)
+
+
+FAR_FIRST = sorted(range(1, INNER), key=hops, reverse=True)
 
 
 def iota(shape, axis):
@@ -133,9 +141,6 @@
     right, left = lax.rem(me + 1, INNER), lax.rem(me + INNER - 1, INNER)
     plane, mine = (me // 8) * 8, lax.rem(me, 8)
     sub, lane = iota((8, 128), 0), iota((8, 128), 1)
-
-    def far_first(k):
-        return lax.rem(me + 1 + lax.rem(15 + k, INNER - 1), INNER)
 
     barrier = pltpu.get_barrier_semaphore()
     others = [(up, right), (up, left), (down, right), (down, left), (up, me), (down, me)]
@@ -341,14 +346,11 @@
     def send_pieces(t):
         r1[t][mine, 0:12] = p1[t, pl.ds(mine * 16, 12)]
 
-        def body(k, carry):
-            to = lax.rem(mine + 1 + k, 8)
+        for k in (4, 3, 5, 2, 6, 1, 7):
+            to = lax.rem(mine + k, 8)
             remote(
                 p1.at[t, pl.ds(to * 16, 12)], r1[t].at[mine, pl.ds(0, 12)], 10 + t, (region, plane + to)
             ).start()
-            return carry
-
-        lax.fori_loop(0, 7, body, 0)
 
     send_pieces(0)
 
@@ -376,6 +378,10 @@
 
     lax.fori_loop(0, 4, coarse_burn, 0, unroll=4)
 
+    z_values(h, 0)
+    for s, pair in enumerate(z_tiles()):
+        for w, tile in enumerate(pair):
+            put_tile(1, s, 4 + w, 0.5 * (get_tile(0, s, 4 + w) + tile))
     for halo in far:
         halo.wait_recv()
 
@@ -402,10 +408,7 @@
         )
         for i, q in enumerate(values):
             fv[2 + e, i] = my[e] * q
-    z_values(h, 0)
-    for s, pair in enumerate(z_tiles()):
-        for w, tile in enumerate(pair):
-            put_tile(1, s, 4 + w, 0.5 * (get_tile(0, s, 4 + w) + tile))
+    for s in range(2):
         for face in range(4):
             put_tile(1, s, face, 0.5 * (get_tile(0, s, face) + xy_tile(face, s)))
     send_pieces(1)
@@ -452,13 +455,10 @@
 
         r2[t][me, 0:6] = piece(my_key)
 
-        def body(k, carry):
-            to = far_first(k)
+        for k in FAR_FIRST:
+            to = lax.rem(me + k, INNER)
             p2[t, to, 0:6] = piece(keys[0, to])
             remote(p2.at[t, to, pl.ds(0, 6)], r2[t].at[me, pl.ds(0, 6)], 12 + t, (region, to)).start()
-            return carry
-
-        lax.fori_loop(0, INNER - 1, body, 0)
 
     pl.semaphore_wait(ready, len(columns))
     send_faces(0)
@@ -510,40 +510,27 @@
     live = [jnp.where(turn < count, 1.0, 0.0) for turn in range(BURN_MAX)]
     group = 16
 
-    def burn(dst):
-        def body(g, carry):
-            at = g * group
-            p = [dst[0, at + i + 1] for i in range(group)]
-            f = [dst[4, at + i + 1] for i in range(group)]
-            for turn in range(BURN_MAX):
-                for i in range(group):
-                    r = pl.reciprocal(fa[at + i] + fb[at + i] * jnp.tanh(p[i]), approx=True)
-                    d = live[turn] * (f[i] - f[i] * r)
-                    f[i] = f[i] - d
-                    p[i] = p[i] + 0.5 * d
+    def burn(dst, at):
+        p = [dst[0, at + i + 1] for i in range(group)]
+        f = [dst[4, at + i + 1] for i in range(group)]
+        for turn in range(BURN_MAX):
             for i in range(group):
-                dst[0, at + i + 1] = p[i]
-                dst[4, at + i + 1] = f[i]
-            return carry
-
-        lax.fori_loop(0, 32 // group, body, 0)
+                r = pl.reciprocal(fa[at + i] + fb[at + i] * jnp.tanh(p[i]), approx=True)
+                d = live[turn] * (f[i] - f[i] * r)
+                f[i] = f[i] - d
+                p[i] = p[i] + 0.5 * d
+        for i in range(group):
+            dst[0, at + i + 1] = p[i]
+            dst[4, at + i + 1] = f[i]
 
     add_ghosts(0, f1)
-    burn(f1)
+    for at in range(0, 32, group):
+        burn(f1, at)
     fine_hydro(f1, f0)
     add_ghosts(1, f0)
-    burn(f0)
-
-    for j in range(8):
-        stores.append(
-            pltpu.make_async_copy(
-                f0.at[:, pl.ds(1, 32), j], fine_out.at[:, :, pl.ds(j * 128, 128)], lsem.at[2 + j]
-            )
-        )
-        stores[-1].start()
     pick_m = ((lane % 32) // 16) * 64 + 2 * (lane % 16)
 
-    def means(a, carry):
+    def means(a):
         for i in range(5):
             tile = zero
             for g in range(4):
@@ -553,18 +540,28 @@
                 q = q + lanes(q, -32)
                 tile = jnp.where(q4 == g, take(q, pick_m), tile)
             mb[pl.ds(a * 64 + i, 8, stride=8)] = 0.125 * tile
-        return carry
-
-    lax.fori_loop(0, 4, means, 0, unroll=2)
-
+
+    def send_mean(to):
+        remote(mb.at[pl.ds(to * 8, 5)], r3.at[me, pl.ds(0, 5)], 14, (region, to)).start()
+
+    for half in range(2):
+        burn(f0, 16 * half)
+        means(2 * half)
+        means(2 * half + 1)
+        for k in range(8, 24):
+            to = 16 * half + lax.rem(me + k, 16)
+            if k != 16:
+                send_mean(to)
+            else:
+                pl.when(me != to)(functools.partial(send_mean, to))
     r3[me, 0:5] = mb[pl.ds(me * 8, 5)]
-
-    def send_mean(k, carry):
-        to = far_first(k)
-        remote(mb.at[pl.ds(to * 8, 5)], r3.at[me, pl.ds(0, 5)], 14, (region, to)).start()
-        return carry
-
-    lax.fori_loop(0, INNER - 1, send_mean, 0)
+    for j in range(8):
+        stores.append(
+            pltpu.make_async_copy(
+                f0.at[:, pl.ds(1, 32), j], fine_out.at[:, :, pl.ds(j * 128, 128)], lsem.at[2 + j]
+            )
+        )
+        stores[-1].start()
     wait_all(r3.at[pl.ds(0, 31), pl.ds(0, 5)], rsem.at[14])
 
     def pick_pair(to):
@@ -575,13 +572,10 @@
     stores.append(pltpu.make_async_copy(p4.at[me], r4.at[me], lsem.at[1]))
     stores[-1].start()
 
-    def send_pair(k, carry):
-        to = far_first(k)
+    for k in FAR_FIRST:
+        to = lax.rem(me + k, INNER)
         pick_pair(to)
         remote(p4.at[to], r4.at[me], 15, (region, to)).start()
-        return carry
-
-    lax.fori_loop(0, INNER - 1, send_pair, 0)
 
     for halo in near + far:
         halo.wait_send()

time: 40.5 us -> 39.3 us (0.970)
  Pallas kernels: 39.1 us -> 37.9 us
    pallas_call x1, Pallas kernels: 36.2 us -> 35 us  [per_device(): pl.pallas_call(kernel, out_shape=(jax.ShapeDtypeStruct((5, 256, 128), F32...]
where the time goes in v3:
time: 39.3 us; the launch traced here: 39.1 us
  Pallas kernels  37.9 us (96%)
  between operations  1.29 us (3%)
    pallas_call x1, Pallas kernels, per_device(): pl.pallas_call(kernel, out_shape=(jax.ShapeDtypeStruct((5, 256, 128), F32...  35 us
    pallas_call x1, Pallas kernels, per_device(): pl.pallas_call(place, out_shape=(jax.ShapeDtypeStruct((5, 256, 128), F32)...  2.85 us

profile of v3, /device:TPU:1, one launch (start us, length us, event | category | flops | bytes accessed | tf_op | source)
XLA Modules:
  0.0 39.1 jit_solution(13428084886301341976)
XLA Ops:
  1.3 35.0 %reactive_step.1 = (f32[5,256,128]{2,1,0:T(8,128)}, f32[5,32,1024]{2,1,0:T(8,128)}, f32[32,10,128]{2,1,0:T(8,128)}, s32[8,128]{1,0:T(8,128)}) custom-call(f32[5,256,128]{2,1,0:T(8,128)} %bitcast.6, f32[5,32,1024]{2,1,0:T(8,128)} %bitcast.7, f32[256,128]{1,0:T(8,128)} %bitcast.8, f32[32,1024]{1,0:T(8,128)} %bitcast.9, s32[1,32]{1,0:T(1,128)} %parents.1, ...), custom_call_target="tpu_custom_call" | custom-call | tf_op jit(solution)/shard_map/reactive_step/pallas_call | solution.py:636
  36.3 2.8 %place.1 = (f32[5,256,128]{2,1,0:T(8,128)}, f32[5,32,1024]{2,1,0:T(8,128)}) custom-call(f32[5,256,128]{2,1,0:T(8,128)} %get-tuple-element.8.stepped, f32[32,10,128]{2,1,0:T(8,128)} %get-tuple-element.9.means, f32[5,32,1024]{2,1,0:T(8,128)} %get-tuple-element.10.fine, s32[8,128]{1,0:T(8,128)} %get-tuple-element.11.table), custom_call_target="tpu_custom_call" | custom-call | tf_op jit(solution)/shard_map/place/pallas_call | solution.py:696

commit v4 on v3

--- a/solution.py
+++ b/solution.py
@@ -143,21 +143,30 @@
     sub, lane = iota((8, 128), 0), iota((8, 128), 1)
 
     barrier = pltpu.get_barrier_semaphore()
-    others = [(up, right), (up, left), (down, right), (down, left), (up, me), (down, me)]
+    has_x = [region > 0, region < REGIONS - 1]
+    has_y = [me > 0, me < INNER - 1]
+    side_x, side_y = (down, up), (left, right)
     columns = [(region, lax.rem(me + 8 * k, INNER)) for k in (2, 1, 3)]
-    outside = [jnp.where(mine == 7, 1, 0), jnp.where(mine == 0, 1, 0)]
-    for other in others + columns:
-        pl.semaphore_signal(barrier, inc=1, device_id=other, device_id_type=MESH)
+    greeted = [(True, other) for other in columns]
+    for e in range(2):
+        greeted.append((has_x[e], (side_x[e], me)))
+        greeted.append((has_y[e] & (mine == 7 * e), (region, side_y[e])))
+        for d in range(2):
+            greeted.append((has_x[e] & has_y[d], (side_x[e], side_y[d])))
     for k in range(1, 8):
-        pl.semaphore_signal(
-            barrier, inc=1, device_id=(region, plane + lax.rem(mine + k, 8)), device_id_type=MESH
-        )
-    for e, other in enumerate((right, left)):
-
-        @pl.when(outside[e] == 1)
-        def _():
-            pl.semaphore_signal(barrier, inc=1, device_id=(region, other), device_id_type=MESH)
-
+        greeted.append((True, (region, plane + lax.rem(mine + k, 8))))
+
+    def hello(to):
+        pl.semaphore_signal(barrier, inc=1, device_id=to, device_id_type=MESH)
+
+    expected = 0
+    for exists, to in greeted:
+        if exists is True:
+            hello(to)
+            expected = expected + 1
+        else:
+            pl.when(exists)(functools.partial(hello, to))
+            expected = expected + jnp.where(exists, 1, 0)
     loads = [
         pltpu.make_async_copy(coarse, c.at[:, pl.ds(16, 256)], lsem.at[0]),
         pltpu.make_async_copy(crate, cr, lsem.at[1]),
@@ -192,33 +201,58 @@
             ds[n, i : i + 1] = c[i, 16 + at : 17 + at]
         ds[n, 5:8] = jnp.zeros((3, 128), F32)
 
-    pl.semaphore_wait(barrier, len(others) + len(columns) + 7 + outside[0] + outside[1])
+    for e in range(2):
+
+        @pl.when(~has_x[e])
+        def _():
+            xh[e] = jnp.zeros(xh.shape[1:], F32)
+            xr[e] = jnp.zeros(xr.shape[1:], F32)
+
+        @pl.when(~has_y[e])
+        def _():
+            yh[e] = jnp.zeros(yh.shape[1:], F32)
+
+        for d in range(2):
+
+            @pl.when(~(has_x[e] & has_y[d]))
+            def _():
+                dr[2 * e + d] = jnp.zeros((8, 128), F32)
+
+    pl.semaphore_wait(barrier, expected)
 
     def remote(src, dst, n, to):
         return pltpu.make_async_remote_copy(
             src_ref=src, dst_ref=dst, send_sem=ssem.at[n], recv_sem=rsem.at[n], device_id=to, device_id_type=MESH
         )
 
-    near = [
-        remote(c.at[:, pl.ds(16 + 240, 16)], xh.at[0, 0], 0, (up, me)),
-        remote(c.at[:, pl.ds(16, 16)], xh.at[1, 0], 1, (down, me)),
-        remote(ys.at[0, 0, pl.ds(0, 5)], yh.at[0, 0, pl.ds(0, 5)], 2, (region, right)),
-        remote(ys.at[1, 0, pl.ds(0, 5)], yh.at[1, 0, pl.ds(0, 5)], 3, (region, left)),
-    ]
-    far = [
-        remote(ds.at[0], dr.at[0], 4, (up, right)),
-        remote(ds.at[1], dr.at[1], 5, (up, left)),
-        remote(ds.at[2], dr.at[2], 6, (down, right)),
-        remote(ds.at[3], dr.at[3], 7, (down, left)),
-        remote(cr.at[pl.ds(240, 16)], xr.at[0], 8, (up, me)),
-        remote(cr.at[pl.ds(0, 16)], xr.at[1], 9, (down, me)),
-        remote(c.at[:, pl.ds(16 + 224, 16)], xh.at[0, 1], 16, (up, me)),
-        remote(c.at[:, pl.ds(32, 16)], xh.at[1, 1], 17, (down, me)),
-        remote(ys.at[0, 1], yh.at[0, 1], 18, (region, right)),
-        remote(ys.at[1, 1], yh.at[1, 1], 19, (region, left)),
-    ]
-    for halo in near + far:
-        halo.start()
+    near, far = [], []
+    for e in range(2):
+        o = 1 - e
+        near.append((remote(c.at[:, pl.ds(16 + 240 * o, 16)], xh.at[e, 0], e, (side_x[o], me)), has_x[o], has_x[e]))
+        near.append(
+            (
+                remote(ys.at[e, 0, pl.ds(0, 5)], yh.at[e, 0, pl.ds(0, 5)], 2 + e, (region, side_y[o])),
+                has_y[o],
+                has_y[e],
+            )
+        )
+        far.append((remote(cr.at[pl.ds(240 * o, 16)], xr.at[e], 8 + e, (side_x[o], me)), has_x[o], has_x[e]))
+        far.append(
+            (remote(c.at[:, pl.ds(32 + 208 * o, 16)], xh.at[e, 1], 16 + e, (side_x[o], me)), has_x[o], has_x[e])
+        )
+        far.append((remote(ys.at[e, 1], yh.at[e, 1], 18 + e, (region, side_y[o])), has_y[o], has_y[e]))
+    for n in range(4):
+        e, d = n // 2, n % 2
+        far.insert(
+            n,
+            (
+                remote(ds.at[n], dr.at[n], 4 + n, (side_x[1 - e], side_y[1 - d])),
+                has_x[1 - e] & has_y[1 - d],
+                has_x[e] & has_y[d],
+            ),
+        )
+    for halo, sends, _ in near + far:
+        pl.when(sends)(halo.start)
     for other in columns:
         pl.semaphore_signal(ready, inc=1, device_id=other, device_id_type=MESH)
 
@@ -321,10 +355,10 @@
         for w, tile in enumerate(pair):
             put_tile(0, s, 4 + w, tile)
 
-    for halo in near:
-        halo.wait_recv()
-    mx = [jnp.where(region > 0, 1.0, 0.0), jnp.where(region < REGIONS - 1, 1.0, 0.0)]
-    my = [jnp.where(me > 0, 1.0, 0.0), jnp.where(me < INNER - 1, 1.0, 0.0)]
+    for halo, _, arrives in near:
+        pl.when(arrives)(halo.wait_recv)
+    mx = [jnp.where(exists, 1.0, 0.0) for exists in has_x]
+    my = [jnp.where(exists, 1.0, 0.0) for exists in has_y]
 
     def near_x(e):
         return [xh[e, 0, i] for i in range(5)]
@@ -382,8 +416,8 @@
     for s, pair in enumerate(z_tiles()):
         for w, tile in enumerate(pair):
             put_tile(1, s, 4 + w, 0.5 * (get_tile(0, s, 4 + w) + tile))
-    for halo in far:
-        halo.wait_recv()
+    for halo, _, arrives in far:
+        pl.when(arrives)(halo.wait_recv)
 
     def own_rows(axis, e):
         if axis == 0:
@@ -458,6 +492,8 @@
         for k in FAR_FIRST:
             to = lax.rem(me + k, INNER)
             p2[t, to, 0:6] = piece(keys[0, to])
+        for k in FAR_FIRST:
+            to = lax.rem(me + k, INNER)
             remote(p2.at[t, to, pl.ds(0, 6)], r2[t].at[me, pl.ds(0, 6)], 12 + t, (region, to)).start()
 
     pl.semaphore_wait(ready, len(columns))
@@ -575,10 +611,12 @@
     for k in FAR_FIRST:
         to = lax.rem(me + k, INNER)
         pick_pair(to)
+    for k in FAR_FIRST:
+        to = lax.rem(me + k, INNER)
         remote(p4.at[to], r4.at[me], 15, (region, to)).start()
 
-    for halo in near + far:
-        halo.wait_send()
+    for halo, sends, _ in near + far:
+        pl.when(sends)(halo.wait_send)
     for t in range(2):
         wait_all(r1[t].at[pl.ds(0, 7), pl.ds(0, 12)], ssem.at[10 + t])
         wait_all(r2[t].at[pl.ds(0, INNER - 1), pl.ds(0, 6)], ssem.at[12 + t])

time: 39.3 us -> 37.7 us (0.959)
  Pallas kernels: 37.9 us -> 36.2 us
    pallas_call x1, Pallas kernels: 35 us -> 33.4 us  [per_device(): pl.pallas_call(kernel, out_shape=(jax.ShapeDtypeStruct((5, 256, 128), F32...]
where the time goes in v4:
time: 37.7 us; the launch traced here: 37.5 us
  Pallas kernels  36.2 us (96%)
  between operations  1.29 us (3%)
    pallas_call x1, Pallas kernels, per_device(): pl.pallas_call(kernel, out_shape=(jax.ShapeDtypeStruct((5, 256, 128), F32...  33.4 us
    pallas_call x1, Pallas kernels, per_device(): pl.pallas_call(place, out_shape=(jax.ShapeDtypeStruct((5, 256, 128), F32)...  2.85 us

profile of v4, /device:TPU:1, one launch (start us, length us, event | category | flops | bytes accessed | tf_op | source)
XLA Modules:
  0.0 37.5 jit_solution(10705144831314623492)
XLA Ops:
  1.3 33.4 %reactive_step.1 = (f32[5,256,128]{2,1,0:T(8,128)}, f32[5,32,1024]{2,1,0:T(8,128)}, f32[32,10,128]{2,1,0:T(8,128)}, s32[8,128]{1,0:T(8,128)}) custom-call(f32[5,256,128]{2,1,0:T(8,128)} %bitcast.6, f32[5,32,1024]{2,1,0:T(8,128)} %bitcast.7, f32[256,128]{1,0:T(8,128)} %bitcast.8, f32[32,1024]{1,0:T(8,128)} %bitcast.9, s32[1,32]{1,0:T(1,128)} %parents.1, ...), custom_call_target="tpu_custom_call" | custom-call | tf_op jit(solution)/shard_map/reactive_step/pallas_call | solution.py:674
  34.7 2.8 %place.1 = (f32[5,256,128]{2,1,0:T(8,128)}, f32[5,32,1024]{2,1,0:T(8,128)}) custom-call(f32[5,256,128]{2,1,0:T(8,128)} %get-tuple-element.8.stepped, f32[32,10,128]{2,1,0:T(8,128)} %get-tuple-element.9.means, f32[5,32,1024]{2,1,0:T(8,128)} %get-tuple-element.10.fine, s32[8,128]{1,0:T(8,128)} %get-tuple-element.11.table), custom_call_target="tpu_custom_call" | custom-call | tf_op jit(solution)/shard_map/place/pallas_call | solution.py:734

commit v5 on v4

--- a/solution.py
+++ b/solution.py
@@ -131,8 +131,8 @@
 
 
 def kernel(
-    coarse, fine, crate, frate, parents, steps, h_out, fine_out, r4, table_out,
-    c, h, cr, xh, xr, ys, yh, ds, dr, fv, zv, table, keys, p1, r1a, r1b, p2, r2a, r2b, f0, f1, fa, fb, fr, gt, ey,
+    coarse, fine, crate, frate, parents, steps, h, fine_out, r4, covers,
+    c, cr, xh, xr, ys, yh, ds, dr, fv, zv, table, keys, p1, r1a, r1b, p2, r2a, r2b, f0, f1, fa, fb, fr, gt, ey,
     mb, r3, p4, pv, sv, ssem, rsem, lsem, tsem, ready,
 ):
     r1, r2 = (r1a, r1b), (r2a, r2b)
@@ -147,14 +147,13 @@
     has_y = [me > 0, me < INNER - 1]
     side_x, side_y = (down, up), (left, right)
     columns = [(region, lax.rem(me + 8 * k, INNER)) for k in (2, 1, 3)]
-    greeted = [(True, other) for other in columns]
+    greeted = [(has_x[e] & has_y[d], (side_x[e], side_y[d])) for e in range(2) for d in range(2)]
     for e in range(2):
         greeted.append((has_x[e], (side_x[e], me)))
         greeted.append((has_y[e] & (mine == 7 * e), (region, side_y[e])))
-        for d in range(2):
-            greeted.append((has_x[e] & has_y[d], (side_x[e], side_y[d])))
-    for k in range(1, 8):
+    for k in (4, 3, 5, 2, 6, 1, 7):
         greeted.append((True, (region, plane + lax.rem(mine + k, 8))))
+    greeted = greeted + [(True, other) for other in columns]
 
     def hello(to):
         pl.semaphore_signal(barrier, inc=1, device_id=to, device_id_type=MESH)
@@ -177,7 +176,7 @@
         cut = pl.ds(j * 128, 128)
         loads.append(pltpu.make_async_copy(fine.at[:, :, cut], f0.at[:, pl.ds(1, 32), j], lsem.at[2 + j]))
         loads.append(pltpu.make_async_copy(frate.at[:, cut], fr.at[:, j], lsem.at[10 + j]))
-    for load in loads:
+    for load in loads[:3]:
         load.start()
 
     zero = jnp.zeros((8, 128), F32)
@@ -253,6 +252,8 @@
         )
     for halo, sends, _ in near + far:
         pl.when(sends)(halo.start)
+    for load in loads[3:]:
+        load.start()
     for other in columns:
         pl.semaphore_signal(ready, inc=1, device_id=other, device_id_type=MESH)
 
@@ -277,8 +278,6 @@
         jnp.broadcast_to(key_row, (8, 128)),
         jnp.where(sub == 1, jnp.broadcast_to(patch_row, (8, 128)), jnp.broadcast_to(layer_row, (8, 128))),
     )
-    keep = pltpu.make_async_copy(table, table_out, lsem.at[18])
-    keep.start()
     look = pltpu.make_async_copy(table, keys, tsem)
     look.start()
 
@@ -297,6 +296,8 @@
 
     look.wait()
     slots = [keys[2, 2 * me], keys[2, 2 * me + 1]]
+    for s in range(2):
+        covers[8 * s : 8 * s + 8] = jnp.where(lane // 16 == slots[s], 1, 0)
     my_key = keys[0, me]
 
     side = lane % 2
@@ -319,7 +320,7 @@
             zv[3, pl.ds(at, 16)] = f * jnp.where(low, NB * (1 + ADV[2]), NB * (1 - ADV[2]))
             return carry
 
-        lax.fori_loop(0, 16, body, 0, unroll=4)
+        lax.fori_loop(0, 16, body, 0, unroll=8)
 
     def z_tiles():
         def body(x, tiles):
@@ -332,7 +333,7 @@
                         tiles[s * 2 + v // 2] = jnp.where(here, take(q, picks[s]), tiles[s * 2 + v // 2])
             return tuple(tiles)
 
-        tiles = lax.fori_loop(0, 16, body, (zero,) * 4, unroll=8)
+        tiles = lax.fori_loop(0, 16, body, (zero,) * 4, unroll=16)
         return [[tiles[s * 2 + w] * inside[s] for w in range(2)] for s in range(2)]
 
     def xy_tile(face, s):
@@ -446,8 +447,6 @@
         for face in range(4):
             put_tile(1, s, face, 0.5 * (get_tile(0, s, face) + xy_tile(face, s)))
     send_pieces(1)
-    stores = [pltpu.make_async_copy(h, h_out, lsem.at[0])]
-    stores[0].start()
 
     for load in loads[3:]:
         load.wait()
@@ -473,7 +472,7 @@
                 dst[i, x + 1] = q
             return carry
 
-        lax.fori_loop(0, 32, body, 0, unroll=8)
+        lax.fori_loop(0, 32, body, 0, unroll=16)
 
     fine_hydro(f0, f1)
 
@@ -499,6 +498,7 @@
     pl.semaphore_wait(ready, len(columns))
     send_faces(0)
     send_faces(1)
+    stores = []
 
     q4, z = lane // 32, lane % 32
     edge_y = jnp.where((lane < 32) & (sub == 0) | (lane >= 96) & (sub == 7), 1.0, 0.0)
@@ -541,7 +541,7 @@
                 dst[i, 2 * x + 2] = dst[i, 2 * x + 2] + add[i]
             return carry
 
-        lax.fori_loop(0, 16, body, 0, unroll=8)
+        lax.fori_loop(0, 16, body, 0, unroll=16)
 
     live = [jnp.where(turn < count, 1.0, 0.0) for turn in range(BURN_MAX)]
     group = 16
@@ -591,6 +591,23 @@
             else:
                 pl.when(me != to)(functools.partial(send_mean, to))
     r3[me, 0:5] = mb[pl.ds(me * 8, 5)]
+
+    wait_all(r3.at[pl.ds(0, 31), pl.ds(0, 5)], rsem.at[14])
+
+    def pick_pair(to):
+        for s in range(2):
+            p4[to, 5 * s : 5 * s + 5] = r3[keys[1, 2 * to + s], 0:5]
+
+    pick_pair(me)
+    r4[me, 0:10] = p4[me]
+
+    for k in FAR_FIRST:
+        to = lax.rem(me + k, INNER)
+        pick_pair(to)
+    for k in FAR_FIRST:
+        to = lax.rem(me + k, INNER)
+        remote(p4.at[to], r4.at[me, pl.ds(0, 10)], 15, (region, to)).start()
+
     for j in range(8):
         stores.append(
             pltpu.make_async_copy(
@@ -598,22 +615,6 @@
             )
         )
         stores[-1].start()
-    wait_all(r3.at[pl.ds(0, 31), pl.ds(0, 5)], rsem.at[14])
-
-    def pick_pair(to):
-        for s in range(2):
-            p4[to, 5 * s : 5 * s + 5] = r3[keys[1, 2 * to + s], 0:5]
-
-    pick_pair(me)
-    stores.append(pltpu.make_async_copy(p4.at[me], r4.at[me], lsem.at[1]))
-    stores[-1].start()
-
-    for k in FAR_FIRST:
-        to = lax.rem(me + k, INNER)
-        pick_pair(to)
-    for k in FAR_FIRST:
-        to = lax.rem(me + k, INNER)
-        remote(p4.at[to], r4.at[me], 15, (region, to)).start()
 
     for halo, sends, _ in near + far:
         pl.when(sends)(halo.wait_send)
@@ -624,27 +625,15 @@
     wait_all(p4.at[pl.ds(0, 31)], ssem.at[15])
     for store in stores:
         store.wait()
-    keep.wait()
-    wait_all(r4.at[pl.ds(0, 31)], rsem.at[15])
-
-
-def place(stepped, means, fine, table, coarse_out, fine_out, h, m, f, keys, sem):
-    me = lax.axis_index("inner")
-    loads = [
-        pltpu.make_async_copy(means, m.at[:, pl.ds(0, 10)], sem.at[0]),
-        pltpu.make_async_copy(table, keys, sem.at[1]),
-        pltpu.make_async_copy(stepped, h, sem.at[2]),
-    ]
-    move = pltpu.make_async_copy(fine, f, sem.at[3])
-    for load in loads:
-        load.start()
-    move.start()
-    for load in loads:
-        load.wait()
+    wait_all(r4.at[pl.ds(0, 31), pl.ds(0, 10)], rsem.at[15])
+
+
+def place(stepped, means, fine, covers, coarse_out, fine_out, h, sem):
+    stores = [pltpu.make_async_copy(fine, fine_out, sem.at[5])]
+    stores[0].start()
     lane = iota((8, 128), 1)
-    here = [lane // 16 == keys[2, 2 * me + s] for s in range(2)]
-    rows_of = m.reshape(512, 128)
-    stores = []
+    here = [covers[8 * s : 8 * s + 8] > 0 for s in range(2)]
+    rows_of = means.reshape(512, 128)
     for i in range(5):
 
         def body(a, carry):
@@ -652,38 +641,33 @@
             for g in range(4):
                 for odd in range(2):
                     at = pl.ds((a * 4 + g) * 16 + odd, 8, stride=2)
-                    q = h[i, at]
+                    q = stepped[i, at]
                     for s in range(2):
                         q = jnp.where(here[s], take(tiles[s], lane % 16 + (g * 32 + odd * 16)), q)
                     h[i, at] = q
             return carry
 
         lax.fori_loop(0, 4, body, 0, unroll=4)
-        stores.append(pltpu.make_async_copy(h.at[i], coarse_out.at[i], sem.at[4 + i]))
+        stores.append(pltpu.make_async_copy(h.at[i], coarse_out.at[i], sem.at[i]))
         stores[-1].start()
-        if i == 0:
-            move.wait()
-            stores.append(pltpu.make_async_copy(f, fine_out, sem.at[3]))
-            stores[-1].start()
     for store in stores:
         store.wait()
 
 
 def per_device(coarse_state, fine_state, coarse_rate, fine_rate, parents, burn_steps):
-    anywhere = pl.BlockSpec(memory_space=pl.ANY)
-    stepped, fine_mid, means, table = pl.pallas_call(
+    vmem, hbm = pl.BlockSpec(memory_space=pltpu.VMEM), pl.BlockSpec(memory_space=pltpu.HBM)
+    stepped, fine_mid, means, covers = pl.pallas_call(
         kernel,
         out_shape=(
             jax.ShapeDtypeStruct((5, 256, 128), F32),
             jax.ShapeDtypeStruct((5, 32, 1024), F32),
-            jax.ShapeDtypeStruct((32, 10, 128), F32),
-            jax.ShapeDtypeStruct((8, 128), jnp.int32),
+            jax.ShapeDtypeStruct((32, 16, 128), F32),
+            jax.ShapeDtypeStruct((16, 128), jnp.int32),
         ),
-        in_specs=[anywhere] * 6,
-        out_specs=(anywhere,) * 4,
+        in_specs=[hbm] * 6,
+        out_specs=(vmem,) * 4,
         scratch_shapes=[
             pltpu.VMEM((5, 288, 128), F32),
-            pltpu.VMEM((5, 256, 128), F32),
             pltpu.VMEM((256, 128), F32),
             pltpu.VMEM((2, 2, 5, 16, 128), F32),
             pltpu.VMEM((2, 16, 128), F32),
@@ -720,15 +704,20 @@
             pltpu.SemaphoreType.REGULAR,
         ],
         compiler_params=pltpu.CompilerParams(
-            collective_id=0, has_side_effects=True, vmem_limit_bytes=60 * 2**20
+            collective_id=0, has_side_effects=True, vmem_limit_bytes=24 * 2**20
         ),
         name="reactive_step",
     )(
-        coarse_state.reshape(5, 256, 128),
-        fine_state.reshape(5, 32, 1024),
-        coarse_rate.reshape(256, 128),
-        fine_rate.reshape(32, 1024),
-        parents,
+        *(
+            pltpu.with_memory_space_constraint(x, pltpu.HBM)
+            for x in (
+                coarse_state.reshape(5, 256, 128),
+                fine_state.reshape(5, 32, 1024),
+                coarse_rate.reshape(256, 128),
+                fine_rate.reshape(32, 1024),
+                parents,
+            )
+        ),
         burn_steps,
     )
     coarse_new, fine_new = pl.pallas_call(
@@ -737,18 +726,15 @@
             jax.ShapeDtypeStruct((5, 256, 128), F32),
             jax.ShapeDtypeStruct((5, 32, 1024), F32),
         ),
-        in_specs=[anywhere] * 4,
-        out_specs=(anywhere,) * 2,
+        in_specs=[vmem] * 4,
+        out_specs=(hbm,) * 2,
         scratch_shapes=[
             pltpu.VMEM((5, 256, 128), F32),
-            pltpu.VMEM((32, 16, 128), F32),
-            pltpu.VMEM((5, 32, 1024), F32),
-            pltpu.SMEM((8, 128), jnp.int32),
-            pltpu.SemaphoreType.DMA((9,)),
+            pltpu.SemaphoreType.DMA((6,)),
         ],
-        compiler_params=pltpu.CompilerParams(vmem_limit_bytes=60 * 2**20),
+        compiler_params=pltpu.CompilerParams(vmem_limit_bytes=24 * 2**20),
         name="place",
-    )(stepped, means, fine_mid, table)
+    )(stepped, means, fine_mid, covers)
     return coarse_new.reshape(5, 16, 16, 128), fine_new.reshape(1, 5, 32, 1024)
 
 

time: 37.7 us -> 35.3 us (0.936)
  Pallas kernels: 36.2 us -> 33.9 us
    pallas_call x1, Pallas kernels: 2.85 us -> 1.57 us  [per_device(): pl.pallas_call(place, out_shape=(jax.ShapeDtypeStruct((5, 256, 128), F32)...]
    pallas_call x1, Pallas kernels: 33.4 us -> 32.4 us  [per_device(): pl.pallas_call(kernel, out_shape=(jax.ShapeDtypeStruct((5, 256, 128), F32...]
where the time goes in v5:
time: 35.3 us; the launch traced here: 35.2 us
  Pallas kernels  33.9 us (96%)
  between operations  1.29 us (4%)
    pallas_call x1, Pallas kernels, per_device(): pl.pallas_call(kernel, out_shape=(jax.ShapeDtypeStruct((5, 256, 128), F32...  32.4 us
    pallas_call x1, Pallas kernels, per_device(): pl.pallas_call(place, out_shape=(jax.ShapeDtypeStruct((5, 256, 128), F32)...  1.57 us

profile of v5, /device:TPU:1, one launch (start us, length us, event | category | flops | bytes accessed | tf_op | source)
XLA Modules:
  0.0 35.2 jit_solution(10021884381721682148)
XLA Ops:
  1.3 32.4 %reactive_step.1 = (f32[5,256,128]{2,1,0:T(8,128)S(1)}, f32[5,32,1024]{2,1,0:T(8,128)S(1)}, f32[32,16,128]{2,1,0:T(8,128)S(1)}, s32[16,128]{1,0:T(8,128)S(1)}) custom-call(f32[5,256,128]{2,1,0:T(8,128)} %bitcast.6, f32[5,32,1024]{2,1,0:T(8,128)} %bitcast.7, f32[256,128]{1,0:T(8,128)} %bitcast.8, f32[32,1024]{1,0:T(8,128)} %bitcast.9, s32[1,32]{1,0:T(1,128)} %parents.1, ...), custom_call_target="tpu_custom_call" | custom-call | tf_op jit(solution)/shard_map/reactive_step/pallas_call | solution.py:659
  33.6 1.6 %place.1 = (f32[5,256,128]{2,1,0:T(8,128)}, f32[5,32,1024]{2,1,0:T(8,128)}) custom-call(f32[5,256,128]{2,1,0:T(8,128)S(1)} %get-tuple-element.8.stepped, f32[32,16,128]{2,1,0:T(8,128)S(1)} %get-tuple-element.9.means, f32[5,32,1024]{2,1,0:T(8,128)S(1)} %get-tuple-element.10.fine, s32[16,128]{1,0:T(8,128)S(1)} %get-tuple-element.11.covers), custom_call_target="tpu_custom_call" | custom-call | tf_op jit(solution)/shard_map/place/pallas_call | solution.py:723

commit v6 on v5

--- a/solution.py
+++ b/solution.py
@@ -301,8 +301,10 @@
     my_key = keys[0, me]
 
     side = lane % 2
-    code = ((lane % 64) // 4) * 4 + (lane // 64) * 2 + (lane % 4) // 2
-    picks = [lax.rem(jnp.where(side == 0, 16 * s + 127, 16 * s + 16) + 128, 128) for s in slots]
+    first = (lane % 4) // 2 == 0
+    own_slot = jnp.where(first, slots[0], slots[1])
+    pick = lax.rem(jnp.where(side == 0, 16 * own_slot + 127, 16 * own_slot + 16) + 128, 128)
+    spread = ((lane % 64) // 4) * 8 + ((lane % 4) // 2) * 4 + side
     cuts = [16 * jnp.maximum(s, 0) + lane % 16 for s in slots]
     inside = [
         jnp.where(((side == 0) & (s == 0)) | ((side == 1) & (s == 7)), 0.0, 1.0) for s in slots
@@ -328,13 +330,17 @@
             for v in range(4):
                 for odd in range(2):
                     q = zv[v, pl.ds(x * 16 + odd, 8, stride=2)]
-                    here = code == x * 4 + (v % 2) * 2 + odd
-                    for s in range(2):
-                        tiles[s * 2 + v // 2] = jnp.where(here, take(q, picks[s]), tiles[s * 2 + v // 2])
+                    tiles[v] = jnp.where(lane // 4 == x * 2 + odd, take(q, pick), tiles[v])
             return tuple(tiles)
 
         tiles = lax.fori_loop(0, 16, body, (zero,) * 4, unroll=16)
-        return [[tiles[s * 2 + w] * inside[s] for w in range(2)] for s in range(2)]
+        return [
+            [
+                inside[s] * jnp.where(lane < 64, take(tiles[2 * w], spread + 2 * s), take(tiles[2 * w + 1], spread + 2 * s))
+                for w in range(2)
+            ]
+            for s in range(2)
+        ]
 
     def xy_tile(face, s):
         tile = zero
@@ -486,14 +492,11 @@
             pair = r1[t][(key & 15) >> 1]
             return jnp.where((key & 1) == 0, pair[0:6], pair[6:12])
 
-        r2[t][me, 0:6] = piece(my_key)
-
         for k in FAR_FIRST:
             to = lax.rem(me + k, INNER)
             p2[t, to, 0:6] = piece(keys[0, to])
-        for k in FAR_FIRST:
-            to = lax.rem(me + k, INNER)
             remote(p2.at[t, to, pl.ds(0, 6)], r2[t].at[me, pl.ds(0, 6)], 12 + t, (region, to)).start()
+        r2[t][me, 0:6] = piece(my_key)
 
     pl.semaphore_wait(ready, len(columns))
     send_faces(0)
@@ -598,16 +601,13 @@
         for s in range(2):
             p4[to, 5 * s : 5 * s + 5] = r3[keys[1, 2 * to + s], 0:5]
 
-    pick_pair(me)
-    r4[me, 0:10] = p4[me]
-
     for k in FAR_FIRST:
         to = lax.rem(me + k, INNER)
         pick_pair(to)
-    for k in FAR_FIRST:
-        to = lax.rem(me + k, INNER)
         remote(p4.at[to], r4.at[me, pl.ds(0, 10)], 15, (region, to)).start()
 
+    pick_pair(me)
+    r4[me, 0:10] = p4[me]
     for j in range(8):
         stores.append(
             pltpu.make_async_copy(

time: 35.3 us -> 35 us (level)
  no operation moved by 1% of the time
where the time goes in v6:
time: 35 us; the launch traced here: 34.9 us
  Pallas kernels  33.6 us (96%)
  between operations  1.29 us (4%)
    pallas_call x1, Pallas kernels, per_device(): pl.pallas_call(kernel, out_shape=(jax.ShapeDtypeStruct((5, 256, 128), F32...  32 us
    pallas_call x1, Pallas kernels, per_device(): pl.pallas_call(place, out_shape=(jax.ShapeDtypeStruct((5, 256, 128), F32)...  1.57 us

profile of v6, /device:TPU:1, one launch (start us, length us, event | category | flops | bytes accessed | tf_op | source)
XLA Modules:
  0.0 34.9 jit_solution(5981472254715290594)
XLA Ops:
  1.3 32.0 %reactive_step.1 = (f32[5,256,128]{2,1,0:T(8,128)S(1)}, f32[5,32,1024]{2,1,0:T(8,128)S(1)}, f32[32,16,128]{2,1,0:T(8,128)S(1)}, s32[16,128]{1,0:T(8,128)S(1)}) custom-call(f32[5,256,128]{2,1,0:T(8,128)} %bitcast.6, f32[5,32,1024]{2,1,0:T(8,128)} %bitcast.7, f32[256,128]{1,0:T(8,128)} %bitcast.8, f32[32,1024]{1,0:T(8,128)} %bitcast.9, s32[1,32]{1,0:T(1,128)} %parents.1, ...), custom_call_target="tpu_custom_call" | custom-call | tf_op jit(solution)/shard_map/reactive_step/pallas_call | solution.py:659
  33.3 1.6 %place.1 = (f32[5,256,128]{2,1,0:T(8,128)}, f32[5,32,1024]{2,1,0:T(8,128)}) custom-call(f32[5,256,128]{2,1,0:T(8,128)S(1)} %get-tuple-element.8.stepped, f32[32,16,128]{2,1,0:T(8,128)S(1)} %get-tuple-element.9.means, f32[5,32,1024]{2,1,0:T(8,128)S(1)} %get-tuple-element.10.fine, s32[16,128]{1,0:T(8,128)S(1)} %get-tuple-element.11.covers), custom_call_target="tpu_custom_call" | custom-call | tf_op jit(solution)/shard_map/place/pallas_call | solution.py:723

commit v7 on v6

--- a/solution.py
+++ b/solution.py
@@ -100,7 +100,10 @@
     n, r = (1, 2) if axis == 0 else (2, 1)
     row, lane = iota((16, 128), 0), iota((16, 128), 1)
     an, ar, az = ADV[axis], ADV[1 - axis], ADV[2]
-    minus, plus = (own, far) if high else (far, own)
+    beyond, tr, tw, tf = far
+    sn = own[0] + own[n] if high else beyond
+    mn = beyond if high else own[0] - own[n]
+    minus_f, plus_f = (own[4], tf) if high else (tf, own[4])
     p, w, f = near[0], near[3], near[4]
 
     def rd(q, d):
@@ -111,15 +114,14 @@
 
     zd = lambda q: jnp.where(lane == 0, 0.0, lanes(q, 1))
     zu = lambda q: jnp.where(lane == 127, 0.0, lanes(q, -1))
-    sn, mn = minus[0] + minus[n], plus[0] - plus[n]
     sr, mr = rd(p + near[r], dlo[0] + dlo[r]), ru(p - near[r], dhi[0] - dhi[r])
     sz, mz = zd(p + w), zu(p - w)
     hp = (sn + mn) + (sr + mr) + (sz + mz)
     hn = (sn - mn) + (rd(near[n], dlo[n]) + ru(near[n], dhi[n])) + (zd(near[n]) + zu(near[n]))
-    hr = (minus[r] + plus[r]) + (sr - mr) + (zd(near[r]) + zu(near[r]))
-    hw = (minus[3] + plus[3]) + (rd(w, dlo[3]) + ru(w, dhi[3])) + (sz - mz)
+    hr = (own[r] + tr) + (sr - mr) + (zd(near[r]) + zu(near[r]))
+    hw = (own[3] + tw) + (rd(w, dlo[3]) + ru(w, dhi[3])) + (sz - mz)
     hf = (
-        ((1 + an) * minus[4] + (1 - an) * plus[4])
+        ((1 + an) * minus_f + (1 - an) * plus_f)
         + ((1 + ar) * rd(f, dlo[4]) + (1 - ar) * ru(f, dhi[4]))
         + ((1 + az) * zd(f) + (1 - az) * zu(f))
     )
@@ -132,7 +134,7 @@
 
 def kernel(
     coarse, fine, crate, frate, parents, steps, h, fine_out, r4, covers,
-    c, cr, xh, xr, ys, yh, ds, dr, fv, zv, table, keys, p1, r1a, r1b, p2, r2a, r2b, f0, f1, fa, fb, fr, gt, ey,
+    c, cr, xs, xh, xr, ys, yh, ds, dr, fv, zv, table, keys, p1, r1a, r1b, p2, r2a, r2b, f0, f1, fa, fb, fr, gt, ey,
     mb, r3, p4, pv, sv, ssem, rsem, lsem, tsem, ready,
 ):
     r1, r2 = (r1a, r1b), (r2a, r2b)
@@ -193,8 +195,13 @@
             dst = pl.ds(half * 8, 8)
             for i in range(5):
                 ys[side, 0, i, dst] = c[i, pl.ds(16 + half * 128 + near, 8, stride=16)]
-                ys[side, 1, i, dst] = c[i, pl.ds(16 + half * 128 + far, 8, stride=16)]
-            ys[side, 1, 5, dst] = cr[pl.ds(half * 128 + near, 8, stride=16)]
+            p, u, v, w, f = (c[i, pl.ds(16 + half * 128 + far, 8, stride=16)] for i in range(5))
+            for i, q in enumerate((p - v if side else p + v, u, w, f)):
+                ys[side, 1, i, dst] = q
+            p, u, v, w, f = (c[i, pl.ds(16 + far * 16 + half * 8, 8)] for i in range(5))
+            for i, q in enumerate((p - u if side else p + u, v, w, f)):
+                xs[side, i, dst] = q
+            ys[side, 1, 4, dst] = cr[pl.ds(half * 128 + near, 8, stride=16)]
     for n, at in enumerate((255, 240, 15, 0)):
         for i in range(5):
             ds[n, i : i + 1] = c[i, 16 + at : 17 + at]
@@ -237,9 +244,9 @@
         )
         far.append((remote(cr.at[pl.ds(240 * o, 16)], xr.at[e], 8 + e, (side_x[o], me)), has_x[o], has_x[e]))
         far.append(
-            (remote(c.at[:, pl.ds(32 + 208 * o, 16)], xh.at[e, 1], 16 + e, (side_x[o], me)), has_x[o], has_x[e])
+            (remote(xs.at[e], xh.at[e, 1, pl.ds(0, 4)], 16 + e, (side_x[o], me)), has_x[o], has_x[e])
         )
-        far.append((remote(ys.at[e, 1], yh.at[e, 1], 18 + e, (region, side_y[o])), has_y[o], has_y[e]))
+        far.append((remote(ys.at[e, 1, pl.ds(0, 5)], yh.at[e, 1, pl.ds(0, 5)], 18 + e, (region, side_y[o])), has_y[o], has_y[e]))
     for n in range(4):
         e, d = n // 2, n % 2
         far.insert(
@@ -439,13 +446,13 @@
 
     for e in range(2):
         values = ghost_step(
-            near_x(e), [xh[e, 1, i] for i in range(5)], own_rows(0, e), corner(2 * e, my[0]), corner(2 * e + 1, my[1]), xr[e], 0, e == 1
+            near_x(e), [xh[e, 1, i] for i in range(4)], own_rows(0, e), corner(2 * e, my[0]), corner(2 * e + 1, my[1]), xr[e], 0, e == 1
         )
         for i, q in enumerate(values):
             fv[e, i] = mx[e] * q
         values = ghost_step(
-            near_y(e), [yh[e, 1, i] for i in range(5)], own_rows(1, e),
-            corner(e, mx[0]), corner(2 + e, mx[1]), yh[e, 1, 5], 1, e == 1,
+            near_y(e), [yh[e, 1, i] for i in range(4)], own_rows(1, e),
+            corner(e, mx[0]), corner(2 + e, mx[1]), yh[e, 1, 4], 1, e == 1,
         )
         for i, q in enumerate(values):
             fv[2 + e, i] = my[e] * q
@@ -669,6 +676,7 @@
         scratch_shapes=[
             pltpu.VMEM((5, 288, 128), F32),
             pltpu.VMEM((256, 128), F32),
+            pltpu.VMEM((2, 4, 16, 128), F32),
             pltpu.VMEM((2, 2, 5, 16, 128), F32),
             pltpu.VMEM((2, 16, 128), F32),
             pltpu.VMEM((2, 2, 6, 16, 128), F32),

time: 35 us -> 35.2 us (level)
  no operation moved by 1% of the time
where the time goes in v7:
time: 35.2 us; the launch traced here: 35 us
  Pallas kernels  33.7 us (96%)
  between operations  1.29 us (4%)
    pallas_call x1, Pallas kernels, per_device(): pl.pallas_call(kernel, out_shape=(jax.ShapeDtypeStruct((5, 256, 128), F32...  32.2 us
    pallas_call x1, Pallas kernels, per_device(): pl.pallas_call(place, out_shape=(jax.ShapeDtypeStruct((5, 256, 128), F32)...  1.57 us

profile of v7, /device:TPU:1, one launch (start us, length us, event | category | flops | bytes accessed | tf_op | source)
XLA Modules:
  0.0 35.0 jit_solution(10488044344003839712)
XLA Ops:
  1.3 32.2 %reactive_step.1 = (f32[5,256,128]{2,1,0:T(8,128)S(1)}, f32[5,32,1024]{2,1,0:T(8,128)S(1)}, f32[32,16,128]{2,1,0:T(8,128)S(1)}, s32[16,128]{1,0:T(8,128)S(1)}) custom-call(f32[5,256,128]{2,1,0:T(8,128)} %bitcast.6, f32[5,32,1024]{2,1,0:T(8,128)} %bitcast.7, f32[256,128]{1,0:T(8,128)} %bitcast.8, f32[32,1024]{1,0:T(8,128)} %bitcast.9, s32[1,32]{1,0:T(1,128)} %parents.1, ...), custom_call_target="tpu_custom_call" | custom-call | tf_op jit(solution)/shard_map/reactive_step/pallas_call | solution.py:666
  33.5 1.6 %place.1 = (f32[5,256,128]{2,1,0:T(8,128)}, f32[5,32,1024]{2,1,0:T(8,128)}) custom-call(f32[5,256,128]{2,1,0:T(8,128)S(1)} %get-tuple-element.8.stepped, f32[32,16,128]{2,1,0:T(8,128)S(1)} %get-tuple-element.9.means, f32[5,32,1024]{2,1,0:T(8,128)S(1)} %get-tuple-element.10.fine, s32[16,128]{1,0:T(8,128)S(1)} %get-tuple-element.11.covers), custom_call_target="tpu_custom_call" | custom-call | tf_op jit(solution)/shard_map/place/pallas_call | solution.py:731
